TPU v7x, 512 devices: a whole 4x8x8 slice. The times are simulated.
512 devices in a mesh: img: 8 (over x, core), dev: 64 (over z, y).
Axes of the slice: x: 4, y: 8, z: 8, core: 2. Of those that a mesh axis runs over, the one named last changes fastest.
Arguments:
- params: float32 [59, 1048576], P(None, ('img', 'dev')), may hold values from -6 to 2.5, as said below
- first_moment: float32 [59, 1048576], P(None, ('img', 'dev')), may hold values from -0.12 to 0.12
- second_moment: float32 [59, 1048576], P(None, ('img', 'dev')), may hold values from 0.001 to 0.1
- send_blocks: int32 [512, 512], P(('img', 'dev')), may hold values from 0 to 511, as said below
- tile_blocks: int32 [8, 64, 512], P('img', 'dev'), may hold values from 0 to 511, as said below
- tile_live: int32 [8, 512], P('img', 'dev'), may hold values from 32 to 64
- depth_order: int32 [8, 512, 256], P('img', 'dev'), may hold values from 0 to 255, each once within a row
- tile_where: int32 [8, 512], P('img', 'dev'), may hold values from 0 to 511, as said below
- target: float32 [8, 512, 768], P('img', 'dev'), may hold values from 0 to 1
- camera: float32 [8, 12], P('img'), may hold values from -0.2 to 6, as said below
Outputs:
- new_params: float32 [59, 1048576], P(None, ('img', 'dev'))
- new_first: float32 [59, 1048576], P(None, ('img', 'dev'))
- new_second: float32 [59, 1048576], P(None, ('img', 'dev'))
Inputs may be any that keep to these rules, and one draw needn't show every extreme that they name: `send_blocks`: an owner sends a different block to each renderer. `tile_blocks`: each renderer's list names every owner once. `tile_where`: each image's tile slots render every tile of the image once. `params`: positions lie within [-2.5, 2.5], the quaternion's real part within [1, 2]. `camera`: the view matrix lies within 0.05 of the identity entrywise, the translation's third entry within [5, 6].
All inputs are finite; a program needn't handle non-finite values.
Results may differ from a plain program's by a relative error of at most 0.0003.
Values sent between devices are 32-bit elements; how exact they have to be, the bound alone decides.
A program may use at most 64 MiB of HBM per device.

v0:
```python
import jax
import jax.numpy as jnp
from jax import lax
from jax.sharding import PartitionSpec as P

TILES_ACROSS = 32


HARMONIC_ZERO = 0.28209479177387814
HARMONIC_ONE = 0.4886025119029199
HARMONIC_TWO = (
    1.0925484305920792,
    -1.0925484305920792,
    0.31539156525252005,
    -1.0925484305920792,
    0.5462742152960396,
)
HARMONIC_THREE = (
    -0.5900435899266435,
    2.890611442640554,
    -0.4570457994644658,
    0.3731763325901154,
    -0.4570457994644658,
    1.445305721320277,
    -0.5900435899266435,
)


def harmonics(dir_x, dir_y, dir_z):
    square_x = dir_x * dir_x
    square_y = dir_y * dir_y
    square_z = dir_z * dir_z
    return [
        HARMONIC_ZERO + 0.0 * dir_x,
        -HARMONIC_ONE * dir_y,
        HARMONIC_ONE * dir_z,
        -HARMONIC_ONE * dir_x,
        HARMONIC_TWO[0] * dir_x * dir_y,
        HARMONIC_TWO[1] * dir_y * dir_z,
        HARMONIC_TWO[2] * (2.0 * square_z - square_x - square_y),
        HARMONIC_TWO[3] * dir_x * dir_z,
        HARMONIC_TWO[4] * (square_x - square_y),
        HARMONIC_THREE[0] * dir_y * (3.0 * square_x - square_y),
        HARMONIC_THREE[1] * dir_x * dir_y * dir_z,
        HARMONIC_THREE[2] * dir_y * (4.0 * square_z - square_x - square_y),
        HARMONIC_THREE[3] * dir_z * (2.0 * square_z - 3.0 * square_x - 3.0 * square_y),
        HARMONIC_THREE[4] * dir_x * (4.0 * square_z - square_x - square_y),
        HARMONIC_THREE[5] * dir_z * (square_x - square_y),
        HARMONIC_THREE[6] * dir_x * (square_x - 3.0 * square_y),
    ]


def shade(harmonic_terms, coefficients):
    channels = []
    for channel in range(3):
        total = 0.5 + harmonic_terms[0] * coefficients[channel]
        for coef_id in range(1, 16):
            total = total + harmonic_terms[coef_id] * coefficients[3 * coef_id + channel]
        channels.append(jnp.maximum(total, 0.0))
    return channels


def choose_columns(fetched, slot_list, tile_count, candidates):
    per_tile = slot_list.shape[0] // tile_count
    block_size = candidates // per_tile
    within = jnp.arange(block_size, dtype=jnp.int32)
    columns = (
        slot_list.reshape(tile_count, per_tile)[:, :, None] * block_size + within[None, None, :]
    ).reshape(tile_count, candidates)
    return fetched[:, columns]


def project(chosen, camera, width_tiles, height_tiles):
    matrix = camera[:9].reshape(3, 3)
    translation = camera[9:]
    viewed = [
        matrix[row_id, 0] * chosen[0]
        + matrix[row_id, 1] * chosen[1]
        + matrix[row_id, 2] * chosen[2]
        + translation[row_id]
        for row_id in range(3)
    ]
    inverse_z = 1.0 / viewed[2]
    focal_len = 32.0 * width_tiles
    centre_u = focal_len * viewed[0] * inverse_z + 8.0 * width_tiles
    centre_v = focal_len * viewed[1] * inverse_z + 8.0 * height_tiles
    scales = jnp.exp(chosen[3:6])
    quat_norm = jnp.sqrt(jnp.sum(chosen[6:10] * chosen[6:10], axis=0))
    real_part = chosen[6] / quat_norm
    imag_x = chosen[7] / quat_norm
    imag_y = chosen[8] / quat_norm
    imag_z = chosen[9] / quat_norm
    rot_matrix = [
        [
            1.0 - 2.0 * (imag_y * imag_y + imag_z * imag_z),
            2.0 * (imag_x * imag_y - real_part * imag_z),
            2.0 * (imag_x * imag_z + real_part * imag_y),
        ],
        [
            2.0 * (imag_x * imag_y + real_part * imag_z),
            1.0 - 2.0 * (imag_x * imag_x + imag_z * imag_z),
            2.0 * (imag_y * imag_z - real_part * imag_x),
        ],
        [
            2.0 * (imag_x * imag_z - real_part * imag_y),
            2.0 * (imag_y * imag_z + real_part * imag_x),
            1.0 - 2.0 * (imag_x * imag_x + imag_y * imag_y),
        ],
    ]
    spread = [
        [rot_matrix[row_id][col_id] * scales[col_id] for col_id in range(3)] for row_id in range(3)
    ]
    jacobian = [
        [
            focal_len * inverse_z * matrix[row_id, col_id]
            - focal_len * viewed[row_id] * inverse_z * inverse_z * matrix[2, col_id]
            for col_id in range(3)
        ]
        for row_id in range(2)
    ]
    projected = [
        [
            jacobian[row_id][0] * spread[0][col_id]
            + jacobian[row_id][1] * spread[1][col_id]
            + jacobian[row_id][2] * spread[2][col_id]
            for col_id in range(3)
        ]
        for row_id in range(2)
    ]
    cov_xx = (
        projected[0][0] * projected[0][0]
        + projected[0][1] * projected[0][1]
        + projected[0][2] * projected[0][2]
        + 0.3
    )
    cov_xy = (
        projected[0][0] * projected[1][0]
        + projected[0][1] * projected[1][1]
        + projected[0][2] * projected[1][2]
    )
    cov_yy = (
        projected[1][0] * projected[1][0]
        + projected[1][1] * projected[1][1]
        + projected[1][2] * projected[1][2]
        + 0.3
    )
    determinant = cov_xx * cov_yy - cov_xy * cov_xy
    conic_xx = cov_yy / determinant
    conic_xy = -cov_xy / determinant
    conic_yy = cov_xx / determinant
    opacity = jax.nn.sigmoid(chosen[10])
    distance = jnp.sqrt(viewed[0] * viewed[0] + viewed[1] * viewed[1] + viewed[2] * viewed[2])
    harmonic_terms = harmonics(viewed[0] / distance, viewed[1] / distance, viewed[2] / distance)
    colour = shade(harmonic_terms, chosen[11:])
    return jnp.stack(
        [
            centre_u,
            centre_v,
            conic_xx,
            conic_xy,
            conic_yy,
            opacity,
            colour[0],
            colour[1],
            colour[2],
        ],
        axis=0,
    )


def composite(shown, live_count, depth_rank, tile_place, target, width_tiles, block_size):
    tile_count, candidates = depth_rank.shape
    centre_u = shown[0]
    centre_v = shown[1]
    conic_xx = shown[2]
    conic_xy = shown[3]
    conic_yy = shown[4]
    opacity = shown[5]
    colour = jnp.transpose(shown[6:9], (1, 0, 2))
    pixel_id = jnp.arange(256, dtype=jnp.int32)
    tile_col = tile_place % width_tiles
    tile_row = tile_place // width_tiles
    pixel_x = (tile_col[:, None] * 16 + pixel_id[None, :] % 16).astype(jnp.float32) + 0.5
    pixel_y = (tile_row[:, None] * 16 + pixel_id[None, :] // 16).astype(jnp.float32) + 0.5
    offset_x = pixel_x[:, :, None] - centre_u[:, None, :]
    offset_y = pixel_y[:, :, None] - centre_v[:, None, :]
    exponent = (
        conic_xx[:, None, :] * offset_x * offset_x
        + 2.0 * conic_xy[:, None, :] * offset_x * offset_y
        + conic_yy[:, None, :] * offset_y * offset_y
    )
    live_mask = (
        (jnp.arange(candidates, dtype=jnp.int32) // block_size)[None, :] < live_count[:, None]
    ).astype(jnp.float32)
    alphas = (opacity * live_mask)[:, None, :] * jnp.exp(-0.5 * exponent)
    sorted_alpha = jnp.take_along_axis(alphas, depth_rank[:, None, :], axis=2)
    sorted_colour = jnp.take_along_axis(colour, depth_rank[:, None, :], axis=2)
    log_keep = jnp.log1p(-sorted_alpha)
    before = jnp.cumsum(log_keep, axis=2) - log_keep
    weights = jnp.exp(before) * sorted_alpha
    rendered = jnp.einsum("tpc,tkc->tkp", weights, sorted_colour, precision=lax.Precision.HIGHEST)
    residual = rendered - target.reshape(tile_count, 3, 256)
    return 0.5 * jnp.sum(residual * residual)


def step_rates():
    return jnp.concatenate(
        [
            jnp.full((3,), 0.00016),
            jnp.full((3,), 0.005),
            jnp.full((4,), 0.001),
            jnp.full((1,), 0.05),
            jnp.full((3,), 0.0025),
            jnp.full((45,), 0.000125),
        ]
    ).astype(jnp.float32)


def local(
    params,
    first_moment,
    second_moment,
    send_blocks,
    tile_blocks,
    tile_live,
    depth_order,
    tile_where,
    target,
    camera,
):
    images = lax.axis_size("img")
    devices = lax.axis_size("dev")
    owners = images * devices
    tile_count = depth_order.shape[1]
    candidates = depth_order.shape[2]
    block_size = candidates * tile_count // owners
    values = params.shape[0]
    height_tiles = tile_count * devices // TILES_ACROSS
    within = jnp.arange(block_size, dtype=jnp.int32)
    columns = (send_blocks[0][:, None] * block_size + within[None, :]).reshape(-1)
    outgoing = params[:, columns].reshape(values, images, devices * block_size)
    slot_list = tile_blocks[0, 0]

    def error_from(shown):
        return composite(
            shown, tile_live[0], depth_order[0], tile_where[0], target[0], TILES_ACROSS, block_size
        )

    landed = lax.all_to_all(
        lax.all_to_all(outgoing, "img", split_axis=1, concat_axis=1, tiled=True),
        "dev",
        split_axis=2,
        concat_axis=2,
        tiled=True,
    )
    fetched = landed.reshape(outgoing.shape[0], owners * block_size)

    def error_of(fetched_values):
        chosen = choose_columns(fetched_values, slot_list, tile_count, candidates)
        return error_from(project(chosen, camera[0], TILES_ACROSS, height_tiles))

    sq_error, pullback = jax.vjp(error_of, fetched)
    (grad_fetched,) = pullback(jnp.ones_like(sq_error))
    landed = lax.all_to_all(
        lax.all_to_all(
            grad_fetched.reshape(values, images, devices * block_size),
            "img",
            split_axis=1,
            concat_axis=1,
            tiled=True,
        ),
        "dev",
        split_axis=2,
        concat_axis=2,
        tiled=True,
    )
    arrived = landed.reshape(values, owners * block_size)
    gradient = jnp.zeros_like(params).at[:, columns].add(arrived)
    new_first = 0.9 * first_moment + 0.1 * gradient
    new_second = 0.999 * second_moment + 0.001 * gradient * gradient
    new_params = params - step_rates()[:, None] * new_first / (jnp.sqrt(new_second) + 1e-15)
    return (new_params, new_first, new_second)


def solution(mesh):
    return jax.shard_map(
        local,
        mesh=mesh,
        in_specs=(
            P(None, ("img", "dev")),
            P(None, ("img", "dev")),
            P(None, ("img", "dev")),
            P(("img", "dev"), None),
            P("img", "dev", None),
            P("img", "dev"),
            P("img", "dev", None),
            P("img", "dev"),
            P("img", "dev", None),
            P("img", None),
        ),
        out_specs=(P(None, ("img", "dev")), P(None, ("img", "dev")), P(None, ("img", "dev"))),
        check_vma=False,
    )
```

profile of v0, /device:TPU:8, one launch (start us, length us, event | category | flops | bytes accessed | tf_op | source)
XLA Modules:
  0.0 269.6 jit_solution(11069581508745267222)
XLA Ops:
  3.1 5.5 %gather_fusion = f32[2048,59]{1,0:T(8,128)S(1)} fusion(f32[59,2048]{0,1:T(8,128)S(1)} %copy.1975, s32[2048]{0:T(1024)S(1)} %broadcast_clamp_fusion.1), kind=kCustom, calls=%fused_computation | custom fusion | bytes 974848 | tf_op jit(solution)/shard_map/gather | solution.py:241
  9.7 4.3 %all-to-all-start = ((f32[59,8,256]{2,0,1:T(8,128)}), f32[59,8,256]{2,0,1:T(8,128)S(1)}, u32[]{:S(2)}, u32[]{:S(2)}) async-start(f32[59,8,256]{2,0,1:T(8,128)} %copy.1976), calls=%async_computation | async-start | bytes 1048576 | tf_op jit(solution)/shard_map/all_to_all | solution.py:250
  16.5 7.9 %all-to-all-done = f32[59,8,256]{2,0,1:T(8,128)S(1)} async-done(((f32[59,8,256]{2,0,1:T(8,128)}), f32[59,8,256]{2,0,1:T(8,128)S(1)}, u32[]{:S(2)}, u32[]{:S(2)}) %all-to-all-start) | async-done | bytes 483360 | tf_op jit(solution)/shard_map/all_to_all | solution.py:250
  27.3 17.2 %all-to-all-start.1 = ((f32[64,1,1888]{2,1,0:T(1,128)}), f32[64,1,1888]{2,1,0:T(1,128)S(1)}, u32[]{:S(2)}, u32[]{:S(2)}) async-start(f32[64,1,1888]{2,1,0:T(1,128)} %reshape.1068), calls=%async_computation.1 | async-start | bytes 983040 | tf_op jit(solution)/shard_map/all_to_all | solution.py:249
  48.6 14.3 %all-to-all-done.1 = f32[64,1,1888]{2,1,0:T(1,128)S(1)} async-done(((f32[64,1,1888]{2,1,0:T(1,128)}), f32[64,1,1888]{2,1,0:T(1,128)S(1)}, u32[]{:S(2)}, u32[]{:S(2)}) %all-to-all-start.1) | async-done | bytes 483360 | tf_op jit(solution)/shard_map/all_to_all | solution.py:249
  67.0 5.5 %gather_fusion.1 = f32[2048,59]{1,0:T(8,128)S(1)} fusion(f32[59,2048]{0,1:T(8,128)S(1)} %bitcast.382, s32[2048]{0:T(1024)S(1)} %broadcast_clamp_fusion), kind=kCustom, calls=%fused_computation.1 | custom fusion | bytes 974848 | tf_op jit(solution)/shard_map/jvp()/gather | solution.py:70
  72.9 7.4 %broadcast_maximum_fusion.2 = (f32[1,8,256]{2,1,0:T(8,128)S(1)}, f32[1,8,256]{2,1,0:T(8,128)S(1)}, f32[1,8,256]{2,1,0:T(8,128)S(1)}, f32[1,8,256]{2,1,0:T(8,128)...) fusion(f32[59,8,256]{2,1,0:T(8,128)S(1)} %bitcast.387, ...), kind=kLoop, calls=%fused_computation.464 | loop fusion | flops 210944 | bytes 221232 | tf_op jit(solution)/shard_map/jvp()/max | solution.py:59
  80.9 13.0 %gather_fusion.2 = f32[2048,3]{1,0:T(8,128)S(1)} fusion(f32[8,3,256]{1,2,0:T(8,128)S(1)} %bitcast.408, s32[2048]{0:T(1024)S(1)} %bitcast.376), kind=kCustom, calls=%fused_computation.2 | custom fusion | bytes 65536 | tf_op jit(solution)/shard_map/jvp(jit(take_along_axis))/gather | solution.py:197
  98.0 23.7 %gather_fusion.3 = f32[2048,256]{1,0:T(8,128)} fusion(f32[8,256,256]{1,2,0:T(8,128)S(1)} %fusion.32, s32[2048]{0:T(1024)S(1)} %bitcast.377), kind=kCustom, calls=%fused_computation.3 | custom fusion | bytes 4210688 | tf_op jit(solution)/shard_map/jvp(jit(take_along_axis))/gather | solution.py:196
  121.7 3.3 %fusion.24 = f32[8,256,2,128]{1,0,3,2:T(8,128)S(1)} fusion(f32[8,256,2,128]{1,3,2,0:T(8,128)} %bitcast.378, pred[8,2,128]{0,2,1:T(8,128)(4,1)S(1)} %copy.1983), kind=kOutput, calls=%fused_computation.46 | output fusion | flops 67633152 | bytes 4196352 | tf_op jit(solution)/shard_map/reduce-window
  129.5 2.9 %fusion.227 = f32[8,256,3]{2,1,0:T(8,128)} fusion(f32[8,256,256]{1,2,0:T(8,128)S(1)} %fusion.26, f32[8,3,256]{2,1,0:T(4,128)S(1)} %fusion.28), kind=kOutput, calls=%fused_computation.532 | convolution fusion | flops 18874368 | bytes 2146304 | tf_op jit(solution)/shard_map/transpose(jvp(tpc,tkc->tkp))/dot_general | solution.py:201
  132.4 4.6 %multiply_multiply_fusion.1 = (f32[8,256,256]{1,2,0:T(8,128)}, f32[8,256,256]{1,2,0:T(8,128)}) fusion(f32[8,256,2,128]{1,3,2,0:T(8,128)S(1)} %copy.1985, f32[8,256,256]{1,2,0:T(8,128)S(1)} %bitcast.380, pred[8,256]{1,0:T(8,128)(4,1)S(1)} %compare_and_fusion.1, f32[8,3,256]{2,1,0:T(4,128)S(1)} %fusion.28, f32[8,256,3]{1,2,0:T(4,128)S(1)} %copy.1987), kind=kOutput, calls=%fused_computation.49 | convolution fusion | flops 21501952 | bytes 8439808 | tf_op jit(solution)/shard_map/transpose(jvp(tpc,tkc->tkp))/dot_general | solution.py:201
  137.0 12.8 %scatter_custom_fusion.2 = f32[3,2048]{0,1:T(8,128)} fusion(s32[2048]{0:T(1024)S(1)} %bitcast.421, f32[2048,3]{1,0:T(8,128)} %bitcast.410, f32[]{:T(128)} %constant.94.clone.1), kind=kCustom, calls=%fused_computation.64 | custom fusion | flops 6144 | bytes 25088
  151.3 6.7 %fusion.20 = f32[8,256,2,128]{1,0,3,2:T(8,128)S(1)} fusion(f32[8,256,2,128]{1,3,2,0:T(8,128)} %bitcast.384), kind=kOutput, calls=%fused_computation.41 | output fusion | flops 66584576 | bytes 4194304 | tf_op jit(solution)/shard_map/reduce-window.2
  160.7 3.1 %fusion.18 = f32[8,256,256]{1,2,0:T(8,128)} fusion(f32[8,256,2,128]{1,3,2,0:T(8,128)S(1)} %copy.1993, f32[8,256,256]{1,2,0:T(8,128)S(1)} %copy-done.3, f32[8,256,2,128]{1,3,2,0:T(8,128)S(1)} %copy-done.2, f32[8,256,256]{1,2,0:T(8,128)S(1)} %bitcast.381, pred[8,256]{1,0:T(8,128)(4,1)S(1)} %compare_and_fusion.1), kind=kLoop, calls=%fused_computation.38 | loop fusion | flops 6291456 | bytes 10487808 | tf_op jit(solution)/shard_map/transpose(jvp())/add_any | solution.py:198
  163.8 12.5 %scatter_custom_fusion.3 = f32[2048,256]{1,0:T(8,128)S(1)} fusion(s32[2048]{0:T(1024)S(1)} %bitcast.422, f32[2048,256]{1,0:T(8,128)} %bitcast.407, f32[]{:T(128)} %constant.94.clone.1), kind=kCustom, calls=%fused_computation.54 | custom fusion | flops 524288 | bytes 2097664
  178.3 4.1 %fusion.4 = (f32[8,256]{1,0:T(8,128)S(1)}, f32[8,256]{1,0:T(8,128)S(1)}, f32[8,256]{1,0:T(8,128)S(1)}, f32[8,256]{1,0:T(8,128)S(1)}, f32[8,256]{1,0:T(8,128)S(1)}, /*index=5*/f32[8,256]{1,0:T(8,128)S(1)}) fusion(f32[8,256,256]{1,2,0:T(8,128)S(1)} %multiply_multiply_fusion, f32[8,256]{1,0:T(8,128)S(1)} %get-tuple-element.180, ...), kind=kLoop, calls=%fused_computation.23 | loop fusion | flops 17289216 | bytes 4300800 | tf_op jit(solution)/shard_map/transpose(jvp())/reduce_sum | solution.py:186
  184.7 5.6 %broadcast_multiply_fusion = (f32[1,8,256]{2,1,0:T(8,128)S(1)}, f32[1,8,256]{2,1,0:T(8,128)S(1)}, f32[1,8,256]{2,1,0:T(8,128)S(1)}, f32[1,8,256]{2,1,0:T(8,128)S...) fusion(f32[]{:T(128)} %bitcast.18, ...), kind=kLoop, calls=%fused_computation.465 | loop fusion | flops 669696 | bytes 761892 | tf_op jit(solution)/shard_map/transpose(jvp())/mul | solution.py:79
  191.6 2.5 broadcast_multiply_fusion.3
  195.2 2.6 broadcast_multiply_fusion.6
  199.8 11.7 %scatter_custom_fusion = f32[59,2048]{0,1:T(8,128)S(1)} fusion(s32[2048]{0:T(1024)S(1)} %bitcast.419, f32[2048,59]{1,0:T(8,128)S(1)} %bitcast.411, f32[]{:T(128)} %constant.94.clone.1), kind=kCustom, calls=%fused_computation.70 | custom fusion | flops 120832 | bytes 483332 | tf_op jit(solution)/shard_map/transpose(jvp())/scatter-add | solution.py:70
  211.9 13.0 %all_to_all.20 = f32[59,8,256]{2,0,1:T(8,128)S(1)} all-to-all(f32[59,8,256]{2,0,1:T(8,128)S(1)} %copy.1995), channel_id=1, replica_groups=mesh['img'=8,'dev'=64] {'img'}, dimensions={1} | all-to-all | bytes 966656 | tf_op jit(solution)/shard_map/all_to_all | solution.py:265
  227.0 23.4 %all_to_all.21 = f32[64,1,1888]{2,1,0:T(1,128)S(1)} all-to-all(f32[64,1,1888]{2,1,0:T(1,128)S(1)} %reshape.1070), channel_id=1, replica_groups=mesh['img'=8,'dev'=64] {'dev'}, dimensions={0} | all-to-all | bytes 966656 | tf_op jit(solution)/shard_map/all_to_all | solution.py:264
  254.9 11.7 %scatter_custom_fusion.1 = f32[59,2048]{0,1:T(8,128)S(1)} fusion(s32[2048]{0:T(1024)S(1)} %bitcast.417, f32[2048,59]{1,0:T(8,128)S(1)} %copy.1998, f32[]{:T(128)} %constant.94.clone.1), kind=kCustom, calls=%fused_computation.68 | custom fusion | flops 120832 | bytes 483332 | tf_op jit(solution)/shard_map/scatter-add | solution.py:278
  (138 shorter events, 44.8 us)
Async XLA Ops:
  8.5 5.5 %copy-start.8 = (f32[1,12]{1,0:T(1,128)S(1)}, f32[1,12]{1,0:T(1,128)}, u32[]{:S(2)}) copy-start(f32[1,12]{1,0:T(1,128)} %param.19) | copy-start | bytes 148
  8.5 6.3 %copy-start.10 = (s32[1,1,512]{2,1,0:T(1,128)S(1)}, s32[1,1,512]{2,1,0:T(1,128)}, u32[]{:S(2)}) copy-start(s32[1,1,512]{2,1,0:T(1,128)} %param.14) | copy-start | bytes 6148
  8.6 7.0 %copy-start.6 = (s32[1,8,256]{2,1,0:T(8,128)S(1)}, s32[1,8,256]{2,1,0:T(8,128)}, u32[]{:S(2)}) copy-start(s32[1,8,256]{2,1,0:T(8,128)} %param.16) | copy-start | bytes 24580
  8.6 7.1 %copy-start.11 = (s32[2]{0:T(128)S(1)}, s32[2]{0:T(128)}, u32[]{:S(2)}) copy-start(s32[2]{0:T(128)} %constant.356) | copy-start | bytes 28
  8.6 7.1 %copy-start.12 = (s32[2]{0:T(128)S(1)}, s32[2]{0:T(128)}, u32[]{:S(2)}) copy-start(s32[2]{0:T(128)} %constant.353) | copy-start | bytes 28
  9.7 14.7 %all-to-all-start = ((f32[59,8,256]{2,0,1:T(8,128)}), f32[59,8,256]{2,0,1:T(8,128)S(1)}, u32[]{:S(2)}, u32[]{:S(2)}) async-start(f32[59,8,256]{2,0,1:T(8,128)} %copy.1976), calls=%async_computation | async-start | bytes 1048576 | tf_op jit(solution)/shard_map/all_to_all | solution.py:250
  16.4 31.9 %copy-start.7 = (f32[1,8,768]{2,1,0:T(8,128)S(1)}, f32[1,8,768]{2,1,0:T(8,128)}, u32[]{:S(2)}) copy-start(f32[1,8,768]{2,1,0:T(8,128)} %param.18) | copy-start | bytes 73732
  16.5 32.0 %copy-start.14 = (s32[1,8]{1,0:T(1,128)S(1)}, s32[1,8]{1,0:T(1,128)}, u32[]{:S(2)}) copy-start(s32[1,8]{1,0:T(1,128)} %param.17) | copy-start | bytes 100
  27.3 35.7 %all-to-all-start.1 = ((f32[64,1,1888]{2,1,0:T(1,128)}), f32[64,1,1888]{2,1,0:T(1,128)S(1)}, u32[]{:S(2)}, u32[]{:S(2)}) async-start(f32[64,1,1888]{2,1,0:T(1,128)} %reshape.1068), calls=%async_computation.1 | async-start | bytes 983040 | tf_op jit(solution)/shard_map/all_to_all | solution.py:249
  72.9 21.3 %copy-start.9 = (s32[1,8]{1,0:T(1,128)S(1)}, s32[1,8]{1,0:T(1,128)}, u32[]{:S(2)}) copy-start(s32[1,8]{1,0:T(1,128)} %param.15) | copy-start | bytes 100
  125.3 1.6 copy-start
  125.9 6.4 %copy-start.1 = (f32[8,256,2,128]{1,3,2,0:T(8,128)}, f32[8,256,2,128]{1,3,2,0:T(8,128)S(1)}, u32[]{:S(2)}) copy-start(f32[8,256,2,128]{1,3,2,0:T(8,128)S(1)} %copy.1985) | copy-start | bytes 6291460
  158.5 1.6 copy-start.2
  158.5 2.2 copy-start.3
  254.5 12.5 %copy-start.4 = (f32[59,2048]{1,0:T(8,128)S(1)}, f32[59,2048]{1,0:T(8,128)}, u32[]{:S(2)}) copy-start(f32[59,2048]{1,0:T(8,128)} %param.10) | copy-start | bytes 1449988
  254.5 12.5 %copy-start.5 = (f32[59,2048]{1,0:T(8,128)S(1)}, f32[59,2048]{1,0:T(8,128)}, u32[]{:S(2)}) copy-start(f32[59,2048]{1,0:T(8,128)} %param.11) | copy-start | bytes 1449988
  254.5 12.5 %copy-start.13 = (f32[59]{0:T(128)S(1)}, f32[59]{0:T(128)}, u32[]{:S(2)}) copy-start(f32[59]{0:T(128)} %constant.85.clone.1) | copy-start | bytes 712
where the time goes:
time: 274 us; the launch traced here: 270 us
  other arithmetic  105 us (38%)
  local copies, waits for them, and re-layouts  70.1 us (26%)
  blocking collectives  36.5 us (13%)
  waiting for transfers between devices  22.2 us (8%)
  starting transfers between devices  21.5 us (8%)
  matrix products  8.55 us (3%)
  between operations  5.38 us (2%)
    unnamed x7, other arithmetic  25.5 us
    gather x1, local copies, waits for them, and re-layouts, composite(): sorted_alpha = jnp.take_along_axis(alphas, depth_rank[:, None, :], axis=2)  23.7 us
    all_to_all x1, blocking collectives, local(): lax.all_to_all(lax.all_to_all(grad_fetched.reshape(values, images, device...  23.4 us
    all_to_all x1, starting transfers between devices, local(): lax.all_to_all(lax.all_to_all(outgoing, 'img', split_axis=1, concat_axis=...  17.2 us
    all_to_all x1, waiting for transfers between devices, local(): lax.all_to_all(lax.all_to_all(outgoing, 'img', split_axis=1, concat_axis=...  14.3 us
    gather x2, local copies, waits for them, and re-layouts, composite(): sorted_colour = jnp.take_along_axis(colour, depth_rank[:, None, :], axis=2)  13.4 us
    all_to_all x1, blocking collectives, local(): lax.all_to_all(grad_fetched.reshape(values, images, devices * block_size)...  13 us
    scatter-add x1, other arithmetic, choose_columns(): return fetched[:, columns]  11.7 us
  transfers between devices with their start and end apart: 2, of which 2 were waited for; matrix products, arithmetic and copies ran while one was open for 1% of the time, Pallas kernels for 0%

commit v1 on v0

v1 whole, which is shorter than its diff:
```python
import functools

import jax
import jax.numpy as jnp
from jax import lax
from jax.experimental import pallas as pl
from jax.experimental.pallas import tpu as pltpu
from jax.sharding import PartitionSpec as P

F32, BF16 = jnp.float32, jnp.bfloat16
LOG2E = 1.4426950408889634
FOCAL = 1024.0
CENTRE_U, CENTRE_V = 256.0, 128.0

HARMONIC_ZERO = 0.28209479177387814
HARMONIC_ONE = 0.4886025119029199
HARMONIC_TWO = (
    1.0925484305920792,
    -1.0925484305920792,
    0.31539156525252005,
    -1.0925484305920792,
    0.5462742152960396,
)
HARMONIC_THREE = (
    -0.5900435899266435,
    2.890611442640554,
    -0.4570457994644658,
    0.3731763325901154,
    -0.4570457994644658,
    1.445305721320277,
    -0.5900435899266435,
)


def harmonics(dir_x, dir_y, dir_z):
    square_x = dir_x * dir_x
    square_y = dir_y * dir_y
    square_z = dir_z * dir_z
    return [
        -HARMONIC_ONE * dir_y,
        HARMONIC_ONE * dir_z,
        -HARMONIC_ONE * dir_x,
        HARMONIC_TWO[0] * dir_x * dir_y,
        HARMONIC_TWO[1] * dir_y * dir_z,
        HARMONIC_TWO[2] * (2.0 * square_z - square_x - square_y),
        HARMONIC_TWO[3] * dir_x * dir_z,
        HARMONIC_TWO[4] * (square_x - square_y),
        HARMONIC_THREE[0] * dir_y * (3.0 * square_x - square_y),
        HARMONIC_THREE[1] * dir_x * dir_y * dir_z,
        HARMONIC_THREE[2] * dir_y * (4.0 * square_z - square_x - square_y),
        HARMONIC_THREE[3] * dir_z * (2.0 * square_z - 3.0 * square_x - 3.0 * square_y),
        HARMONIC_THREE[4] * dir_x * (4.0 * square_z - square_x - square_y),
        HARMONIC_THREE[5] * dir_z * (square_x - square_y),
        HARMONIC_THREE[6] * dir_x * (square_x - 3.0 * square_y),
    ]


def project(values, cam):
    m = [[cam[3 * r + c] for c in range(3)] for r in range(3)]
    viewed = [m[r][0] * values[0] + m[r][1] * values[1] + m[r][2] * values[2] + cam[9 + r] for r in range(3)]
    inverse_z = 1.0 / viewed[2]
    centre_u = FOCAL * viewed[0] * inverse_z + CENTRE_U
    centre_v = FOCAL * viewed[1] * inverse_z + CENTRE_V
    scales = [jnp.exp(values[3 + c]) for c in range(3)]
    norm = jnp.sqrt(values[6] * values[6] + values[7] * values[7] + values[8] * values[8] + values[9] * values[9])
    inverse_norm = 1.0 / norm
    w, x, y, z = (values[6 + c] * inverse_norm for c in range(4))
    rot = [
        [1.0 - 2.0 * (y * y + z * z), 2.0 * (x * y - w * z), 2.0 * (x * z + w * y)],
        [2.0 * (x * y + w * z), 1.0 - 2.0 * (x * x + z * z), 2.0 * (y * z - w * x)],
        [2.0 * (x * z - w * y), 2.0 * (y * z + w * x), 1.0 - 2.0 * (x * x + y * y)],
    ]
    focal_z = FOCAL * inverse_z
    jac = [[focal_z * (m[r][c] - viewed[r] * inverse_z * m[2][c]) for c in range(3)] for r in range(2)]
    proj = [
        [(jac[r][0] * rot[0][c] + jac[r][1] * rot[1][c] + jac[r][2] * rot[2][c]) * scales[c] for c in range(3)]
        for r in range(2)
    ]
    cov_xx = proj[0][0] * proj[0][0] + proj[0][1] * proj[0][1] + proj[0][2] * proj[0][2] + 0.3
    cov_xy = proj[0][0] * proj[1][0] + proj[0][1] * proj[1][1] + proj[0][2] * proj[1][2]
    cov_yy = proj[1][0] * proj[1][0] + proj[1][1] * proj[1][1] + proj[1][2] * proj[1][2] + 0.3
    inverse_det = 1.0 / (cov_xx * cov_yy - cov_xy * cov_xy)
    log_opacity = -jnp.log(1.0 + jnp.exp(-values[10]))
    inverse_distance = 1.0 / jnp.sqrt(viewed[0] * viewed[0] + viewed[1] * viewed[1] + viewed[2] * viewed[2])
    terms = harmonics(*[viewed[c] * inverse_distance for c in range(3)])
    colour = []
    for ch in range(3):
        total = 0.5 + HARMONIC_ZERO * values[11 + ch]
        for k in range(1, 16):
            total = total + terms[k - 1] * values[11 + 3 * k + ch]
        colour.append(jnp.maximum(total, 0.0))
    return [centre_u, centre_v, cov_yy * inverse_det, -cov_xy * inverse_det, cov_xx * inverse_det, log_opacity] + colour


def iota(shape, dim):
    return lax.broadcasted_iota(jnp.int32, shape, dim)


def one_hot(truth):
    return jnp.where(truth, 1.0, 0.0).astype(BF16)


def pieces(x, count):
    out = []
    for _ in range(count - 1):
        part = x.astype(BF16)
        out.append(part)
        x = x - part.astype(F32)
    out.append(x.astype(BF16))
    return out


def nn(a, b):
    return lax.dot_general(a, b, (((1,), (0,)), ((), ())), preferred_element_type=F32)


def nt(a, b):
    return lax.dot_general(a, b, (((1,), (1,)), ((), ())), preferred_element_type=F32)


def fold(x, count):
    rows = x.shape[0] // count
    total = x[:rows]
    for c in range(1, count):
        total = total + x[c * rows:(c + 1) * rows]
    return total


def owner_tables(send_ref, params_ref, pick, image_of, par3):
    send = send_ref[...]

    def chunk(g, carry):
        lanes = pl.ds(pl.multiple_of(g * 256, 256), 256)
        pick[lanes, :] = one_hot(iota((256, 512), 0) // 4 + g * 64 == send)
        return carry

    lax.fori_loop(0, 8, chunk, 0)
    image_row = jnp.broadcast_to((iota((8, 512), 1) // 64).astype(F32), (8, 512)).astype(BF16)
    images = nt(image_row, pick[...])
    for g in range(8):
        image_of[g:g + 1, :] = images[0:1, 256 * g:256 * (g + 1)]
        par3[:, g, :] = params_ref[:, 256 * g:256 * (g + 1)]


def cameras_of(cam_ref, image_of):
    image = image_of[...]
    masks = [image == float(i) for i in range(8)]
    cams = cam_ref[...]
    out = []
    for t in range(12):
        value = jnp.zeros((8, 256), F32)
        for i in range(8):
            value = jnp.where(masks[i], cams[i:i + 1, t:t + 1], value)
        out.append(value)
    return out


def owner_forward(cam_ref, pick, image_of, par3, shown3, put):
    shown = project([par3[c] for c in range(59)], cameras_of(cam_ref, image_of))
    for q in range(9):
        shown3[q] = shown[q]
    for q in range(9, 16):
        shown3[q] = jnp.zeros((8, 256), F32)
    within = iota((16, 256), 1) % 4
    total = jnp.zeros((192, 512), F32)
    for g in range(8):
        rows = []
        for b in range(4):
            rows.append(jnp.where(within == b, shown3[:, g, :], 0.0))
        rows = jnp.concatenate(rows, axis=0)
        total = total + nn(jnp.concatenate(pieces(rows, 3), axis=0), pick[256 * g:256 * (g + 1), :])
    sums = fold(total, 3)
    put(jnp.transpose(jnp.concatenate([sums, jnp.zeros((64, 512), F32)], axis=0)))


def owner_gradient(got, cam_ref, pick, image_of, par3, shown3, grad3):
    rows = jnp.transpose(got)[0:64]
    parts = jnp.concatenate(pieces(rows, 3), axis=0)
    within = iota((16, 256), 1) % 4
    for g in range(8):
        spread = fold(nt(parts, pick[256 * g:256 * (g + 1), :]), 3)
        total = jnp.zeros((16, 256), F32)
        for b in range(4):
            total = total + jnp.where(within == b, spread[16 * b:16 * (b + 1)], 0.0)
        shown3[:, g, :] = total
    values = [par3[c] for c in range(59)]
    cams = cameras_of(cam_ref, image_of)
    _, pullback = jax.vjp(lambda v: project(v, cams), values)
    (grads,) = pullback([shown3[q] for q in range(9)])
    for c in range(59):
        grad3[c] = grads[c]


def renderer_tables(lists_ref, order_ref, where_ref, live_ref, listed, sort, place, tri):
    listed[...] = one_hot(iota((512, 512), 0) == lists_ref[...])

    def one_tile(n, carry):
        order = order_ref[pl.ds(n, 1), :]
        key = (order % 4) * 128 + (n % 2) * 64 + order // 4
        sort[n] = one_hot(iota((512, 256), 0) == key)
        return carry

    lax.fori_loop(0, 8, one_tile, 0)
    lane = iota((8, 512), 1)
    tile = lane // 64
    where = jnp.zeros((8, 512), jnp.int32)
    live = jnp.zeros((8, 512), jnp.int32)
    for n in range(8):
        where = jnp.where(tile == n, where_ref[0, n], where)
        live = jnp.where(tile == n, live_ref[0, n], live)
    place[0] = (where % 32 * 16 + 8).astype(F32)
    place[1] = (where // 32 * 16 + 8).astype(F32)
    place[2] = jnp.where(lane % 64 < live, 1.0, 0.0)
    tri[...] = one_hot(iota((256, 256), 0) < iota((256, 256), 1))


def monomials(pixel, term):
    x = (pixel % 16).astype(F32) - 7.5
    y = (pixel // 16).astype(F32) - 7.5
    out = jnp.zeros(pixel.shape, F32)
    for t, value in enumerate((jnp.ones_like(x), x, y, x * x, x * y, y * y)):
        out = jnp.where(term == t, value, out)
    return out.astype(BF16)


def render(got, listed, sort, place, tri, target_ref, tile3, coef3, grad3, put):
    rows = jnp.transpose(got)[0:64]
    tiles = fold(nn(jnp.concatenate(pieces(rows, 3), axis=0), listed[...]), 3)
    for b in range(4):
        tile3[:, b, :] = tiles[16 * b:16 * (b + 1)]
    centre_x, centre_y, live = place[0, 0:4], place[1, 0:4], place[2, 0:4]

    def geometry():
        u, v, cxx, cxy, cyy, log_op = (tile3[q, 0:4] for q in range(6))
        return u - centre_x, v - centre_y, cxx, cxy, cyy, log_op

    u, v, cxx, cxy, cyy, log_op = geometry()
    a, b2, c2 = -0.5 * LOG2E * cxx, -LOG2E * cxy, -0.5 * LOG2E * cyy
    constant = a * u * u + b2 * u * v + c2 * v * v + LOG2E * log_op
    coefs = [
        jnp.where(live > 0.0, constant, -1e5),
        jnp.where(live > 0.0, -2.0 * a * u - b2 * v, 0.0),
        jnp.where(live > 0.0, -2.0 * c2 * v - b2 * u, 0.0),
        jnp.where(live > 0.0, a, 0.0),
        jnp.where(live > 0.0, b2, 0.0),
        jnp.where(live > 0.0, c2, 0.0),
    ] + [tile3[q, 0:4] for q in range(6, 9)]
    for c in range(9):
        coef3[c, 0:4] = coefs[c]
    for c in range(9, 16):
        coef3[c, 0:4] = jnp.zeros((4, 512), F32)
    grad3[...] = jnp.zeros(grad3.shape, F32)
    power = monomials(iota((256, 48), 0), iota((256, 48), 1) % 16)
    moment = monomials(iota((16, 256), 1), iota((16, 256), 0))
    lower = tri[...]

    for n in range(8):
        pair = slice(128 * (n // 2), 128 * (n // 2) + 128)
        mine = jnp.concatenate([coef3[:, b, pair] for b in range(4)], axis=1)
        sorted_parts = nn(jnp.concatenate(pieces(mine, 3), axis=0), sort[n])
        front = fold(sorted_parts, 3)
        q2 = nn(power, sorted_parts.astype(BF16))
        alpha = jnp.exp2(q2)
        log_keep = jnp.log(1.0 - alpha)
        hi, lo = pieces(log_keep, 2)
        before = jnp.exp(nn(hi, lower) + nn(lo, lower))
        weight = before * alpha
        w_hi, w_lo = pieces(weight, 2)
        colour = jnp.where(iota((8, 256), 0) < 3, pltpu.roll(front, 10, 0)[0:8], 0.0)
        c_all = jnp.concatenate(pieces(colour, 2), axis=0)
        rendered = fold(nt(c_all, w_hi), 2) + fold(nt(c_all, w_lo), 2)
        wanted = jnp.concatenate([target_ref[n:n + 1, 256 * ch:256 * (ch + 1)] for ch in range(3)] + [jnp.zeros((5, 256), F32)], axis=0)
        residual = rendered - wanted
        down = jnp.transpose(jnp.concatenate([residual, jnp.zeros((120, 256), F32)], axis=0))
        gain = down[:, 0:1] * colour[0:1] + down[:, 1:2] * colour[1:2] + down[:, 2:3] * colour[2:3]
        passed = weight * gain
        hi, lo = pieces(passed, 2)
        behind = nt(hi, lower) + nt(lo, lower)
        change = passed - behind * (alpha * jnp.exp(-log_keep))
        moments = nn(moment, pieces(change, 3)[0]) + nn(moment, pieces(change, 3)[1]) + nn(moment, pieces(change, 3)[2])
        r_all = jnp.concatenate(pieces(residual, 2), axis=0)
        shade = fold(nn(r_all, w_hi), 2) + fold(nn(r_all, w_lo), 2)
        back = jnp.concatenate([moments[0:8], shade], axis=0)
        spread = fold(nt(jnp.concatenate(pieces(back, 3), axis=0), sort[n]), 3)
        for b in range(4):
            grad3[:, b, pair] += spread[:, 128 * b:128 * (b + 1)]

    m0, mx, my, mxx, mxy, myy = (grad3[t, 0:4] for t in range(6))
    u, v, cxx, cxy, cyy, _ = geometry()
    hx, hy = mx - u * m0, my - v * m0
    hxx = mxx - 2.0 * u * mx + u * u * m0
    hxy = mxy - u * my - v * mx + u * v * m0
    hyy = myy - 2.0 * v * my + v * v * m0
    results = [cxx * hx + cxy * hy, cxy * hx + cyy * hy, -0.5 * hxx, -hxy, -0.5 * hyy, m0]
    results += [grad3[8 + ch, 0:4] for ch in range(3)]
    for q in range(9):
        tile3[q, 0:4] = results[q]
    for q in range(9, 16):
        tile3[q, 0:4] = jnp.zeros((4, 512), F32)
    rows = jnp.concatenate([tile3[:, b, :] for b in range(4)], axis=0)
    out = fold(nt(jnp.concatenate(pieces(rows, 3), axis=0), listed[...]), 3)
    put(jnp.transpose(jnp.concatenate([out, jnp.zeros((64, 512), F32)], axis=0)))


def rate_column():
    row = iota((59, 1), 0)
    rate = jnp.full((59, 1), 0.000125, F32)
    for end, value in ((14, 0.0025), (11, 0.05), (10, 0.001), (6, 0.005), (3, 0.00016)):
        rate = jnp.where(row < end, value, rate)
    return rate


def adam(grad3, params_ref, first_ref, second_ref, new_params, new_first, new_second):
    rate = rate_column()
    for g in range(8):
        at = slice(256 * g, 256 * (g + 1))
        gradient = grad3[:, g, :]
        first = 0.9 * first_ref[:, at] + 0.1 * gradient
        second = 0.999 * second_ref[:, at] + 0.001 * gradient * gradient
        new_first[:, at] = first
        new_second[:, at] = second
        new_params[:, at] = params_ref[:, at] - rate * first / (jnp.sqrt(second) + 1e-15)


OWNER_SCRATCH = [
    pltpu.VMEM((2048, 512), BF16),
    pltpu.VMEM((8, 256), F32),
    pltpu.VMEM((59, 8, 256), F32),
    pltpu.VMEM((16, 8, 256), F32),
]
RENDER_SCRATCH = [
    pltpu.VMEM((512, 512), BF16),
    pltpu.VMEM((8, 512, 256), BF16),
    pltpu.VMEM((3, 8, 512), F32),
    pltpu.VMEM((256, 256), BF16),
    pltpu.VMEM((16, 8, 512), F32),
    pltpu.VMEM((16, 8, 512), F32),
    pltpu.VMEM((16, 8, 512), F32),
]


def landed(ref, sem):
    pltpu.make_async_copy(ref, ref, sem).wait()


def step(
    send_ref, params_ref, lists_ref, order_ref, where_ref, live_ref, target_ref, camera_ref, out_ref,
    pick, image_of, par3, shown3, owner3, listed, sort, place, tri, tile3, coef3, grad3,
    cam_row, cams, shown_out, shown_mid, shown_in, back_out, back_mid, back_in, send_sems, recv_sems, own_sem,
):
    i = lax.axis_index("img")
    j = lax.axis_index("dev")
    mesh_ids = pl.DeviceIdType.MESH

    barrier = pltpu.get_barrier_semaphore()
    for s in range(1, 8):
        pl.semaphore_signal(barrier, inc=1, device_id=(lax.rem(i + s, 8), j), device_id_type=mesh_ids)

    @pl.loop(1, 64)
    def _(s):
        pl.semaphore_signal(barrier, inc=1, device_id=(i, lax.rem(j + s, 64)), device_id_type=mesh_ids)

    cam_row[...] = jnp.zeros((8, 128), F32)
    cam_row[0:1, 0:12] = camera_ref[...]
    owner_tables(send_ref, params_ref, pick, image_of, par3)
    pl.semaphore_wait(barrier, 70)

    def to_img(source, target, phase):
        for s in range(1, 8):
            t = lax.rem(i + s, 8)
            pltpu.make_async_remote_copy(
                src_ref=source(t),
                dst_ref=target,
                send_sem=send_sems.at[phase],
                recv_sem=recv_sems.at[phase],
                device_id=(t, j),
                device_id_type=mesh_ids,
            ).start()
        own = pltpu.make_async_copy(source(i), target, own_sem)
        own.start()
        own.wait()

    def to_dev(source, target, phase):
        def one(s, carry):
            t = lax.rem(j + s, 64)
            pltpu.make_async_remote_copy(
                src_ref=source.at[:, t, :],
                dst_ref=target.at[:, j, :],
                send_sem=send_sems.at[phase],
                recv_sem=recv_sems.at[phase],
                device_id=(i, t),
                device_id_type=mesh_ids,
            ).start()
            return carry

        lax.fori_loop(1, 64, one, 0)
        own = pltpu.make_async_copy(source.at[:, j, :], target.at[:, j, :], own_sem)
        own.start()
        own.wait()

    to_img(lambda t: cam_row.at[pl.ds(0, 1)], cams.at[pl.ds(i, 1)], 0)
    landed(cams.at[pl.ds(0, 7)], recv_sems.at[0])

    def put_shown(x):
        shown_out[...] = x.reshape(8, 64, 128)

    owner_forward(cams, pick, image_of, par3, shown3, put_shown)
    to_img(lambda t: shown_out.at[t], shown_mid.at[i], 1)
    renderer_tables(lists_ref, order_ref, where_ref, live_ref, listed, sort, place, tri)
    landed(shown_mid.at[pl.ds(0, 7)], recv_sems.at[1])
    to_dev(shown_mid, shown_in, 2)
    landed(shown_in.at[:, pl.ds(0, 63), :], recv_sems.at[2])

    def put_back(x):
        back_out[...] = x.reshape(8, 64, 128)

    render(shown_in[...].reshape(512, 128), listed, sort, place, tri, target_ref, tile3, coef3, grad3, put_back)
    to_dev(back_out, back_mid, 3)
    landed(back_mid.at[:, pl.ds(0, 63), :], recv_sems.at[3])
    to_img(lambda t: back_mid.at[t], back_in.at[i], 4)
    landed(back_in.at[pl.ds(0, 7)], recv_sems.at[4])
    owner_gradient(back_in[...].reshape(512, 128), cams, pick, image_of, par3, shown3, owner3)
    for g in range(8):
        out_ref[:, 256 * g:256 * (g + 1)] = owner3[:, g, :]
    landed(cams.at[pl.ds(0, 7)], send_sems.at[0])
    landed(shown_out.at[pl.ds(0, 7)], send_sems.at[1])
    landed(shown_mid.at[:, pl.ds(0, 63), :], send_sems.at[2])
    landed(back_out.at[:, pl.ds(0, 63), :], send_sems.at[3])
    landed(back_mid.at[pl.ds(0, 7)], send_sems.at[4])


def local(
    params, first_moment, second_moment, send_blocks, tile_blocks, tile_live, depth_order, tile_where, target, camera
):
    vmem = pl.BlockSpec(memory_space=pltpu.VMEM)
    smem = pl.BlockSpec(memory_space=pltpu.SMEM)
    block = pltpu.VMEM((8, 64, 128), F32)
    gradient = pl.pallas_call(
        step,
        out_shape=jax.ShapeDtypeStruct((59, 2048), F32),
        in_specs=[vmem, vmem, vmem, vmem, smem, smem, vmem, vmem],
        out_specs=vmem,
        scratch_shapes=OWNER_SCRATCH
        + [pltpu.VMEM((59, 8, 256), F32)]
        + RENDER_SCRATCH
        + [pltpu.VMEM((8, 128), F32)] * 2
        + [block] * 6
        + [pltpu.SemaphoreType.DMA((5,)), pltpu.SemaphoreType.DMA((5,)), pltpu.SemaphoreType.DMA],
        compiler_params=pltpu.CompilerParams(collective_id=0, has_side_effects=True, vmem_limit_bytes=40 << 20),
    )(
        send_blocks,
        params,
        tile_blocks.reshape(1, 512),
        depth_order.reshape(8, 256),
        tile_where,
        tile_live,
        target.reshape(8, 768),
        camera,
    )
    new_first = 0.9 * first_moment + 0.1 * gradient
    new_second = 0.999 * second_moment + 0.001 * gradient * gradient
    new_params = params - rate_column() * new_first / (jnp.sqrt(new_second) + 1e-15)
    return new_params, new_first, new_second


def solution(mesh):
    return jax.shard_map(
        local,
        mesh=mesh,
        in_specs=(
            P(None, ("img", "dev")),
            P(None, ("img", "dev")),
            P(None, ("img", "dev")),
            P(("img", "dev"), None),
            P("img", "dev", None),
            P("img", "dev"),
            P("img", "dev", None),
            P("img", "dev"),
            P("img", "dev", None),
            P("img", None),
        ),
        out_specs=(P(None, ("img", "dev")), P(None, ("img", "dev")), P(None, ("img", "dev"))),
        check_vma=False,
    )
```

time: 274 us -> 72.5 us (0.26)
  the two profiles are of different devices: /device:TPU:8 before, /device:TPU:1 now
where the time goes in v1:
time: 72.5 us; the launch traced here: 72.2 us
  Pallas kernels  67.1 us (93%)
  local copies, waits for them, and re-layouts  3.15 us (4%)
  other arithmetic  1.33 us (2%)
    pallas_call x1, Pallas kernels, local(): pl.pallas_call(step, out_shape=jax.ShapeDtypeStruct((59, 2048), F32), in_...  67.1 us
    unnamed x20, local copies, waits for them, and re-layouts  3.15 us

profile of v1, /device:TPU:1, one launch (start us, length us, event | category | flops | bytes accessed | tf_op | source)
XLA Modules:
  0.0 72.2 jit_solution(1001789058514550416)
XLA Ops:
  0.6 0.0 copy-start.4
  0.6 0.0 copy-start.3
  0.7 0.0 copy-start.5
  0.7 0.0 copy-start.6
  0.7 0.0 copy-start.7
  0.7 0.6 copy-done.4
  1.3 0.0 copy-done.3
  1.3 0.0 copy-done.5
  1.3 0.0 copy-done.6
  1.3 0.0 copy-done.7
  1.4 0.0 copy-start
  1.4 1.0 %copy-done = f32[59,2048]{1,0:T(8,128)S(1)} copy-done((f32[59,2048]{1,0:T(8,128)S(1)}, f32[59,2048]{1,0:T(8,128)}, u32[]{:S(2)}) %copy-start) | copy-done | bytes 483352
  2.4 0.0 copy-start.1
  2.4 0.7 %copy-done.1 = f32[1,8,768]{2,1,0:T(8,128)S(1)} copy-done((f32[1,8,768]{2,1,0:T(8,128)S(1)}, f32[1,8,768]{2,1,0:T(8,128)}, u32[]{:S(2)}) %copy-start.1) | copy-done | bytes 24600
  3.1 0.0 copy-start.2
  3.1 0.7 copy-done.2
  3.8 0.0 copy-start.8
  3.8 0.0 copy-start.9
  3.8 67.1 %shard_map.121 = f32[59,2048]{1,0:T(8,128)S(1)} custom-call(s32[1,512]{1,0:T(1,128)S(1)} %copy-done.3, f32[59,2048]{1,0:T(8,128)S(1)} %copy-done, s32[1,512]{1,0:T(1,128)S(1)} %bitcast.5, s32[8,256]{1,0:T(8,128)S(1)} %bitcast.4, s32[1,8]{1,0:T(1,128)S(1)} %copy-done.5, s32[1,8]{1,0:T(1,128)S(1)} %copy-done.6, f32[8,768]{1,0:T(8,128)S(1)} %bitcast.3, ...), custom_call_target="tpu_custom_call" | custom-call | tf_op jit(solution)/shard_map/pallas_call | solution.py:438
  70.9 0.0 copy-done.8
  70.9 0.0 copy-done.9
  70.9 1.3 %divide_subtract_fusion = (f32[59,2048]{1,0:T(8,128)}, f32[59,2048]{1,0:T(8,128)}, f32[59,2048]{1,0:T(8,128)}) fusion(f32[59,2048]{1,0:T(8,128)S(1)} %copy-done, f32[59]{0:T(128)S(1)} %compare_select_fusion.4, f32[59,2048]{1,0:T(8,128)S(1)} %shard_map.121, f32[59,2048]{1,0:T(8,128)S(1)} %copy-done.8, f32[59,2048]{1,0:T(8,128)S(1)} %copy-done.9), kind=kLoop, calls=%fused_computation.2 | loop fusion | flops 1329152 | bytes 3383532 | tf_op jit(solution)/shard_map/sub | solution.py:462
  (1 shorter events, 0.0 us)
Async XLA Ops:
  0.6 0.7 copy-start.4
  0.6 0.7 copy-start.3
  0.7 0.7 copy-start.5
  0.7 0.7 copy-start.6
  0.7 0.7 copy-start.7
  1.4 1.0 %copy-start = (f32[59,2048]{1,0:T(8,128)S(1)}, f32[59,2048]{1,0:T(8,128)}, u32[]{:S(2)}) copy-start(f32[59,2048]{1,0:T(8,128)} %params_ref.1) | copy-start | bytes 1449988
  2.4 0.7 %copy-start.1 = (f32[1,8,768]{2,1,0:T(8,128)S(1)}, f32[1,8,768]{2,1,0:T(8,128)}, u32[]{:S(2)}) copy-start(f32[1,8,768]{2,1,0:T(8,128)} %param.18) | copy-start | bytes 73732
  3.1 0.7 copy-start.2
  3.8 67.1 %copy-start.8 = (f32[59,2048]{1,0:T(8,128)S(1)}, f32[59,2048]{1,0:T(8,128)}, u32[]{:S(2)}) copy-start(f32[59,2048]{1,0:T(8,128)} %param.11) | copy-start | bytes 1449988
  3.8 67.1 %copy-start.9 = (f32[59,2048]{1,0:T(8,128)S(1)}, f32[59,2048]{1,0:T(8,128)}, u32[]{:S(2)}) copy-start(f32[59,2048]{1,0:T(8,128)} %param.12) | copy-start | bytes 1449988

commit v2 on v1

--- a/solution.py
+++ b/solution.py
@@ -126,7 +126,7 @@
     return total
 
 
-def owner_tables(send_ref, params_ref, pick, image_of, par3):
+def owner_tables(send_ref, pick, image_of):
     send = send_ref[...]
 
     def chunk(g, carry):
@@ -139,7 +139,6 @@
     images = nt(image_row, pick[...])
     for g in range(8):
         image_of[g:g + 1, :] = images[0:1, 256 * g:256 * (g + 1)]
-        par3[:, g, :] = params_ref[:, 256 * g:256 * (g + 1)]
 
 
 def cameras_of(cam_ref, image_of):
@@ -191,7 +190,7 @@
         grad3[c] = grads[c]
 
 
-def renderer_tables(lists_ref, order_ref, where_ref, live_ref, listed, sort, place, tri):
+def renderer_tables(lists_ref, order_ref, where_ref, live_ref, target_ref, listed, sort, place, tri, wanted):
     listed[...] = one_hot(iota((512, 512), 0) == lists_ref[...])
 
     def one_tile(n, carry):
@@ -206,12 +205,16 @@
     where = jnp.zeros((8, 512), jnp.int32)
     live = jnp.zeros((8, 512), jnp.int32)
     for n in range(8):
-        where = jnp.where(tile == n, where_ref[0, n], where)
-        live = jnp.where(tile == n, live_ref[0, n], live)
+        where = jnp.where(tile == n, where_ref[0:1, n:n + 1], where)
+        live = jnp.where(tile == n, live_ref[0:1, n:n + 1], live)
     place[0] = (where % 32 * 16 + 8).astype(F32)
     place[1] = (where // 32 * 16 + 8).astype(F32)
     place[2] = jnp.where(lane % 64 < live, 1.0, 0.0)
-    tri[...] = one_hot(iota((256, 256), 0) < iota((256, 256), 1))
+    tri[0] = one_hot(iota((256, 256), 0) < iota((256, 256), 1))
+    tri[1] = one_hot(iota((256, 256), 0) > iota((256, 256), 1))
+    for n in range(8):
+        rows = [target_ref[n:n + 1, 256 * ch:256 * (ch + 1)] for ch in range(3)]
+        wanted[n] = jnp.transpose(jnp.concatenate(rows + [jnp.zeros((125, 256), F32)], axis=0))[:, 0:8]
 
 
 def monomials(pixel, term):
@@ -223,7 +226,7 @@
     return out.astype(BF16)
 
 
-def render(got, listed, sort, place, tri, target_ref, tile3, coef3, grad3, put):
+def render(got, listed, sort, place, tri, wanted, tile3, coef3, grad3, front3, alpha3, weight3, high3, low3, put):
     rows = jnp.transpose(got)[0:64]
     tiles = fold(nn(jnp.concatenate(pieces(rows, 3), axis=0), listed[...]), 3)
     for b in range(4):
@@ -251,36 +254,52 @@
         coef3[c, 0:4] = jnp.zeros((4, 512), F32)
     grad3[...] = jnp.zeros(grad3.shape, F32)
     power = monomials(iota((256, 48), 0), iota((256, 48), 1) % 16)
-    moment = monomials(iota((16, 256), 1), iota((16, 256), 0))
-    lower = tri[...]
+    column = iota((16, 256), 0).astype(F32) - 7.5
+    zero8 = jnp.zeros((8, 256), F32)
 
     for n in range(8):
         pair = slice(128 * (n // 2), 128 * (n // 2) + 128)
         mine = jnp.concatenate([coef3[:, b, pair] for b in range(4)], axis=1)
         sorted_parts = nn(jnp.concatenate(pieces(mine, 3), axis=0), sort[n])
         front = fold(sorted_parts, 3)
-        q2 = nn(power, sorted_parts.astype(BF16))
-        alpha = jnp.exp2(q2)
-        log_keep = jnp.log(1.0 - alpha)
-        hi, lo = pieces(log_keep, 2)
-        before = jnp.exp(nn(hi, lower) + nn(lo, lower))
-        weight = before * alpha
-        w_hi, w_lo = pieces(weight, 2)
-        colour = jnp.where(iota((8, 256), 0) < 3, pltpu.roll(front, 10, 0)[0:8], 0.0)
+        front3[n] = jnp.where(iota((8, 256), 0) < 3, pltpu.roll(front, 10, 0)[0:8], 0.0)
+        alpha = jnp.exp2(nn(power, sorted_parts.astype(BF16)))
+        alpha3[n] = alpha
+        high3[n], low3[n] = pieces(jnp.log(1.0 - alpha), 2)
+    for n in range(8):
+        weight = jnp.exp(nn(high3[n], tri[0]) + nn(low3[n], tri[0])) * alpha3[n]
+        weight3[n] = weight
+        high3[n], low3[n] = pieces(weight, 2)
+    for n in range(8):
+        colour = front3[n]
         c_all = jnp.concatenate(pieces(colour, 2), axis=0)
-        rendered = fold(nt(c_all, w_hi), 2) + fold(nt(c_all, w_lo), 2)
-        wanted = jnp.concatenate([target_ref[n:n + 1, 256 * ch:256 * (ch + 1)] for ch in range(3)] + [jnp.zeros((5, 256), F32)], axis=0)
-        residual = rendered - wanted
-        down = jnp.transpose(jnp.concatenate([residual, jnp.zeros((120, 256), F32)], axis=0))
-        gain = down[:, 0:1] * colour[0:1] + down[:, 1:2] * colour[1:2] + down[:, 2:3] * colour[2:3]
+        both = nt(high3[n], c_all) + nt(low3[n], c_all)
+        residual = both[:, 0:8] + both[:, 8:16] - wanted[n]
+        weight = weight3[n]
+        gain = jnp.zeros((256, 256), F32)
+        shades = []
+        for ch in range(3):
+            gain = gain + residual[:, ch:ch + 1] * colour[ch:ch + 1]
+            shades.append(jnp.sum(residual[:, ch:ch + 1] * weight, axis=0, keepdims=True))
         passed = weight * gain
-        hi, lo = pieces(passed, 2)
-        behind = nt(hi, lower) + nt(lo, lower)
-        change = passed - behind * (alpha * jnp.exp(-log_keep))
-        moments = nn(moment, pieces(change, 3)[0]) + nn(moment, pieces(change, 3)[1]) + nn(moment, pieces(change, 3)[2])
-        r_all = jnp.concatenate(pieces(residual, 2), axis=0)
-        shade = fold(nn(r_all, w_hi), 2) + fold(nn(r_all, w_lo), 2)
-        back = jnp.concatenate([moments[0:8], shade], axis=0)
+        weight3[n] = passed
+        high3[n], low3[n] = pieces(passed, 2)
+        front3[n] = jnp.concatenate(shades + [zero8[0:5]], axis=0)
+    for n in range(8):
+        alpha = alpha3[n]
+        keep = 1.0 - alpha
+        guess = pl.reciprocal(keep, approx=True)
+        inverse = guess * (2.0 - keep * guess)
+        behind = nn(high3[n], tri[1]) + nn(low3[n], tri[1])
+        change = (weight3[n] - behind * (alpha * inverse)).reshape(16, 16, 256)
+        s0, s1, s2 = change[0], -7.5 * change[0], 56.25 * change[0]
+        for y in range(1, 16):
+            s0 = s0 + change[y]
+            s1 = s1 + (y - 7.5) * change[y]
+            s2 = s2 + (y - 7.5) * (y - 7.5) * change[y]
+        moments = [s0, s0 * column, s1, s0 * column * column, s1 * column, s2]
+        back = jnp.concatenate([jnp.sum(m, axis=0, keepdims=True) for m in moments] + [zero8[0:2], front3[n]], axis=0)
+        pair = slice(128 * (n // 2), 128 * (n // 2) + 128)
         spread = fold(nt(jnp.concatenate(pieces(back, 3), axis=0), sort[n]), 3)
         for b in range(4):
             grad3[:, b, pair] += spread[:, 128 * b:128 * (b + 1)]
@@ -332,10 +351,16 @@
     pltpu.VMEM((512, 512), BF16),
     pltpu.VMEM((8, 512, 256), BF16),
     pltpu.VMEM((3, 8, 512), F32),
-    pltpu.VMEM((256, 256), BF16),
+    pltpu.VMEM((2, 256, 256), BF16),
+    pltpu.VMEM((8, 256, 8), F32),
     pltpu.VMEM((16, 8, 512), F32),
     pltpu.VMEM((16, 8, 512), F32),
     pltpu.VMEM((16, 8, 512), F32),
+    pltpu.VMEM((8, 8, 256), F32),
+    pltpu.VMEM((8, 256, 256), F32),
+    pltpu.VMEM((8, 256, 256), F32),
+    pltpu.VMEM((8, 256, 256), BF16),
+    pltpu.VMEM((8, 256, 256), BF16),
 ]
 
 
@@ -344,14 +369,28 @@
 
 
 def step(
-    send_ref, params_ref, lists_ref, order_ref, where_ref, live_ref, target_ref, camera_ref, out_ref,
-    pick, image_of, par3, shown3, owner3, listed, sort, place, tri, tile3, coef3, grad3,
+    params_hbm, send_hbm, lists_hbm, order_hbm, where_hbm, live_hbm, target_hbm, camera_hbm, out_ref,
+    send_ref, lists_ref, order_ref, where_ref, live_ref, target_ref, camera_ref, in_sems,
+    pick, image_of, par3, shown3, owner3,
+    listed, sort, place, tri, wanted, tile3, coef3, grad3, front3, alpha3, weight3, high3, low3,
     cam_row, cams, shown_out, shown_mid, shown_in, back_out, back_mid, back_in, send_sems, recv_sems, own_sem,
 ):
     i = lax.axis_index("img")
     j = lax.axis_index("dev")
     mesh_ids = pl.DeviceIdType.MESH
 
+    loads = [
+        pltpu.make_async_copy(source, target, in_sems.at[c])
+        for c, (source, target) in enumerate(
+            [(camera_hbm, camera_ref), (send_hbm, send_ref)]
+            + [(params_hbm.at[:, pl.ds(256 * g, 256)], par3.at[:, g, :]) for g in range(8)]
+            + [(lists_hbm, lists_ref), (order_hbm, order_ref), (where_hbm, where_ref), (live_hbm, live_ref)]
+            + [(target_hbm, target_ref)]
+        )
+    ]
+    for load in loads:
+        load.start()
+
     barrier = pltpu.get_barrier_semaphore()
     for s in range(1, 8):
         pl.semaphore_signal(barrier, inc=1, device_id=(lax.rem(i + s, 8), j), device_id_type=mesh_ids)
@@ -361,8 +400,10 @@
         pl.semaphore_signal(barrier, inc=1, device_id=(i, lax.rem(j + s, 64)), device_id_type=mesh_ids)
 
     cam_row[...] = jnp.zeros((8, 128), F32)
+    loads[0].wait()
     cam_row[0:1, 0:12] = camera_ref[...]
-    owner_tables(send_ref, params_ref, pick, image_of, par3)
+    loads[1].wait()
+    owner_tables(send_ref, pick, image_of)
     pl.semaphore_wait(barrier, 70)
 
     def to_img(source, target, phase):
@@ -404,9 +445,13 @@
     def put_shown(x):
         shown_out[...] = x.reshape(8, 64, 128)
 
+    for load in loads[2:10]:
+        load.wait()
     owner_forward(cams, pick, image_of, par3, shown3, put_shown)
     to_img(lambda t: shown_out.at[t], shown_mid.at[i], 1)
-    renderer_tables(lists_ref, order_ref, where_ref, live_ref, listed, sort, place, tri)
+    for load in loads[10:]:
+        load.wait()
+    renderer_tables(lists_ref, order_ref, where_ref, live_ref, target_ref, listed, sort, place, tri, wanted)
     landed(shown_mid.at[pl.ds(0, 7)], recv_sems.at[1])
     to_dev(shown_mid, shown_in, 2)
     landed(shown_in.at[:, pl.ds(0, 63), :], recv_sems.at[2])
@@ -414,7 +459,11 @@
     def put_back(x):
         back_out[...] = x.reshape(8, 64, 128)
 
-    render(shown_in[...].reshape(512, 128), listed, sort, place, tri, target_ref, tile3, coef3, grad3, put_back)
+    render(
+        shown_in[...].reshape(512, 128),
+        listed, sort, place, tri, wanted, tile3, coef3, grad3, front3, alpha3, weight3, high3, low3,
+        put_back,
+    )
     to_dev(back_out, back_mid, 3)
     landed(back_mid.at[:, pl.ds(0, 63), :], recv_sems.at[3])
     to_img(lambda t: back_mid.at[t], back_in.at[i], 4)
@@ -433,23 +482,34 @@
     params, first_moment, second_moment, send_blocks, tile_blocks, tile_live, depth_order, tile_where, target, camera
 ):
     vmem = pl.BlockSpec(memory_space=pltpu.VMEM)
-    smem = pl.BlockSpec(memory_space=pltpu.SMEM)
+    whole = pl.BlockSpec(memory_space=pl.ANY)
+    integer = jnp.int32
     block = pltpu.VMEM((8, 64, 128), F32)
     gradient = pl.pallas_call(
         step,
         out_shape=jax.ShapeDtypeStruct((59, 2048), F32),
-        in_specs=[vmem, vmem, vmem, vmem, smem, smem, vmem, vmem],
+        in_specs=[whole] * 8,
         out_specs=vmem,
-        scratch_shapes=OWNER_SCRATCH
+        scratch_shapes=[
+            pltpu.VMEM((1, 512), integer),
+            pltpu.VMEM((1, 512), integer),
+            pltpu.VMEM((8, 256), integer),
+            pltpu.VMEM((1, 8), integer),
+            pltpu.VMEM((1, 8), integer),
+            pltpu.VMEM((8, 768), F32),
+            pltpu.VMEM((1, 12), F32),
+            pltpu.SemaphoreType.DMA((15,)),
+        ]
+        + OWNER_SCRATCH
         + [pltpu.VMEM((59, 8, 256), F32)]
         + RENDER_SCRATCH
         + [pltpu.VMEM((8, 128), F32)] * 2
         + [block] * 6
         + [pltpu.SemaphoreType.DMA((5,)), pltpu.SemaphoreType.DMA((5,)), pltpu.SemaphoreType.DMA],
-        compiler_params=pltpu.CompilerParams(collective_id=0, has_side_effects=True, vmem_limit_bytes=40 << 20),
+        compiler_params=pltpu.CompilerParams(collective_id=0, has_side_effects=True, vmem_limit_bytes=56 << 20),
     )(
+        params,
         send_blocks,
-        params,
         tile_blocks.reshape(1, 512),
         depth_order.reshape(8, 256),
         tile_where,

time: 72.5 us -> 63.3 us (0.87)
  Pallas kernels: 67.1 us -> 59.9 us
  local copies, waits for them, and re-layouts: 3.15 us -> 0.01 us
  other arithmetic: 1.33 us -> 2.52 us
    pallas_call x1, Pallas kernels: 67.1 us -> 59.9 us  [local(): pl.pallas_call(step, out_shape=jax.ShapeDtypeStruct((59, 2048), F32), in_...]
    unnamed x20 -> x4, local copies, waits for them, and re-layouts: 3.15 us -> 0.01 us
    sub x1, other arithmetic: 1.32 us -> 2.51 us  [local(): params - rate_column() * new_first / (jnp.sqrt(new_second) + 1e-15)]
where the time goes in v2:
time: 63.3 us; the launch traced here: 63.1 us
  Pallas kernels  59.9 us (95%)
  other arithmetic  2.52 us (4%)
  between operations  0.68 us (1%)
    pallas_call x1, Pallas kernels, local(): pl.pallas_call(step, out_shape=jax.ShapeDtypeStruct((59, 2048), F32), in_...  59.9 us
    sub x1, other arithmetic, local(): params - rate_column() * new_first / (jnp.sqrt(new_second) + 1e-15)  2.51 us

profile of v2, /device:TPU:1, one launch (start us, length us, event | category | flops | bytes accessed | tf_op | source)
XLA Modules:
  0.0 63.1 jit_solution(17516986994139266976)
XLA Ops:
  0.6 0.0 copy-start
  0.7 0.0 copy-start.1
  0.7 59.9 %shard_map.121 = f32[59,2048]{1,0:T(8,128)} custom-call(f32[59,2048]{1,0:T(8,128)} %params_hbm.1, s32[1,512]{1,0:T(1,128)} %send_hbm.1, s32[1,512]{1,0:T(1,128)} %bitcast.5, s32[8,256]{1,0:T(8,128)} %bitcast.4, s32[1,8]{1,0:T(1,128)} %where_hbm.1, s32[1,8]{1,0:T(1,128)} %live_hbm.1, f32[8,768]{1,0:T(8,128)} %bitcast.3, f32[1,12]{1,0:T(1,128)} %camera_hbm.1), custom_call_target="tpu_custom_call" | custom-call | tf_op jit(solution)/shard_map/pallas_call | solution.py:488
  60.6 0.0 copy-done
  60.6 0.0 copy-done.1
  60.6 2.5 %divide_subtract_fusion = (f32[59,2048]{1,0:T(8,128)}, f32[59,2048]{1,0:T(8,128)}, f32[59,2048]{1,0:T(8,128)}) fusion(f32[59,2048]{1,0:T(8,128)S(1)} %copy-done, f32[59]{0:T(128)S(1)} %compare_select_fusion.4, f32[59,2048]{1,0:T(8,128)} %shard_map.121, f32[59,2048]{1,0:T(8,128)S(1)} %copy-done.1, f32[59,2048]{1,0:T(8,128)} %param.12), kind=kLoop, calls=%fused_computation.2 | loop fusion | flops 1329152 | bytes 3383532 | tf_op jit(solution)/shard_map/sub | solution.py:522
  (1 shorter events, 0.0 us)
Async XLA Ops:
  0.6 60.0 %copy-start = (f32[59,2048]{1,0:T(8,128)S(1)}, f32[59,2048]{1,0:T(8,128)}, u32[]{:S(2)}) copy-start(f32[59,2048]{1,0:T(8,128)} %params_hbm.1) | copy-start | bytes 1449988
  0.7 60.0 %copy-start.1 = (f32[59,2048]{1,0:T(8,128)S(1)}, f32[59,2048]{1,0:T(8,128)}, u32[]{:S(2)}) copy-start(f32[59,2048]{1,0:T(8,128)} %param.11) | copy-start | bytes 1449988

commit v3 on v2

--- a/solution.py
+++ b/solution.py
@@ -118,6 +118,21 @@
     return lax.dot_general(a, b, (((1,), (1,)), ((), ())), preferred_element_type=F32)
 
 
+def paired_rows(x):
+    return jnp.transpose(jnp.concatenate([x[:, 0:256], x[:, 256:512]], axis=0))
+
+
+def unpaired(x):
+    down = jnp.transpose(x)
+    return jnp.concatenate([down[0:64], down[64:128]], axis=1)
+
+
+def exchange_halves(a, b):
+    first = iota(a.shape, len(a.shape) - 1) < 64
+    turned_a, turned_b = pltpu.roll(a, 64, len(a.shape) - 1), pltpu.roll(b, 64, len(b.shape) - 1)
+    return jnp.where(first, a, turned_b), jnp.where(first, turned_a, b)
+
+
 def fold(x, count):
     rows = x.shape[0] // count
     total = x[:rows]
@@ -168,13 +183,11 @@
             rows.append(jnp.where(within == b, shown3[:, g, :], 0.0))
         rows = jnp.concatenate(rows, axis=0)
         total = total + nn(jnp.concatenate(pieces(rows, 3), axis=0), pick[256 * g:256 * (g + 1), :])
-    sums = fold(total, 3)
-    put(jnp.transpose(jnp.concatenate([sums, jnp.zeros((64, 512), F32)], axis=0)))
+    put(paired_rows(fold(total, 3)))
 
 
 def owner_gradient(got, cam_ref, pick, image_of, par3, shown3, grad3):
-    rows = jnp.transpose(got)[0:64]
-    parts = jnp.concatenate(pieces(rows, 3), axis=0)
+    parts = jnp.concatenate(pieces(unpaired(got), 3), axis=0)
     within = iota((16, 256), 1) % 4
     for g in range(8):
         spread = fold(nt(parts, pick[256 * g:256 * (g + 1), :]), 3)
@@ -191,7 +204,8 @@
 
 
 def renderer_tables(lists_ref, order_ref, where_ref, live_ref, target_ref, listed, sort, place, tri, wanted):
-    listed[...] = one_hot(iota((512, 512), 0) == lists_ref[...])
+    spot = iota((512, 512), 0)
+    listed[...] = one_hot(spot // 32 % 8 * 64 + spot // 256 * 32 + spot % 32 == lists_ref[...])
 
     def one_tile(n, carry):
         order = order_ref[pl.ds(n, 1), :]
@@ -227,7 +241,7 @@
 
 
 def render(got, listed, sort, place, tri, wanted, tile3, coef3, grad3, front3, alpha3, weight3, high3, low3, put):
-    rows = jnp.transpose(got)[0:64]
+    rows = unpaired(got)
     tiles = fold(nn(jnp.concatenate(pieces(rows, 3), axis=0), listed[...]), 3)
     for b in range(4):
         tile3[:, b, :] = tiles[16 * b:16 * (b + 1)]
@@ -317,8 +331,7 @@
     for q in range(9, 16):
         tile3[q, 0:4] = jnp.zeros((4, 512), F32)
     rows = jnp.concatenate([tile3[:, b, :] for b in range(4)], axis=0)
-    out = fold(nt(jnp.concatenate(pieces(rows, 3), axis=0), listed[...]), 3)
-    put(jnp.transpose(jnp.concatenate([out, jnp.zeros((64, 512), F32)], axis=0)))
+    put(paired_rows(fold(nt(jnp.concatenate(pieces(rows, 3), axis=0), listed[...]), 3)))
 
 
 def rate_column():
@@ -373,11 +386,19 @@
     send_ref, lists_ref, order_ref, where_ref, live_ref, target_ref, camera_ref, in_sems,
     pick, image_of, par3, shown3, owner3,
     listed, sort, place, tri, wanted, tile3, coef3, grad3, front3, alpha3, weight3, high3, low3,
-    cam_row, cams, shown_out, shown_mid, shown_in, back_out, back_mid, back_in, send_sems, recv_sems, own_sem,
+    cam_row, cams, shown_out, shown_mid, back_send, back_in, shown_send, shown_in, back_out, back_mid, send_sems, recv_sems, own_sem,
 ):
     i = lax.axis_index("img")
     j = lax.axis_index("dev")
     mesh_ids = pl.DeviceIdType.MESH
+
+    barrier = pltpu.get_barrier_semaphore()
+    for s in range(1, 8):
+        pl.semaphore_signal(barrier, inc=1, device_id=(lax.rem(i + s, 8), j), device_id_type=mesh_ids)
+
+    @pl.loop(1, 64)
+    def _(s):
+        pl.semaphore_signal(barrier, inc=1, device_id=(i, lax.rem(j + s, 64)), device_id_type=mesh_ids)
 
     loads = [
         pltpu.make_async_copy(source, target, in_sems.at[c])
@@ -390,20 +411,9 @@
     ]
     for load in loads:
         load.start()
-
-    barrier = pltpu.get_barrier_semaphore()
-    for s in range(1, 8):
-        pl.semaphore_signal(barrier, inc=1, device_id=(lax.rem(i + s, 8), j), device_id_type=mesh_ids)
-
-    @pl.loop(1, 64)
-    def _(s):
-        pl.semaphore_signal(barrier, inc=1, device_id=(i, lax.rem(j + s, 64)), device_id_type=mesh_ids)
-
     cam_row[...] = jnp.zeros((8, 128), F32)
     loads[0].wait()
     cam_row[0:1, 0:12] = camera_ref[...]
-    loads[1].wait()
-    owner_tables(send_ref, pick, image_of)
     pl.semaphore_wait(barrier, 70)
 
     def to_img(source, target, phase):
@@ -425,8 +435,8 @@
         def one(s, carry):
             t = lax.rem(j + s, 64)
             pltpu.make_async_remote_copy(
-                src_ref=source.at[:, t, :],
-                dst_ref=target.at[:, j, :],
+                src_ref=source.at[t],
+                dst_ref=target.at[j],
                 send_sem=send_sems.at[phase],
                 recv_sem=recv_sems.at[phase],
                 device_id=(i, t),
@@ -435,56 +445,79 @@
             return carry
 
         lax.fori_loop(1, 64, one, 0)
-        own = pltpu.make_async_copy(source.at[:, j, :], target.at[:, j, :], own_sem)
+        own = pltpu.make_async_copy(source.at[j], target.at[j], own_sem)
         own.start()
         own.wait()
 
     to_img(lambda t: cam_row.at[pl.ds(0, 1)], cams.at[pl.ds(i, 1)], 0)
+    loads[1].wait()
+    owner_tables(send_ref, pick, image_of)
     landed(cams.at[pl.ds(0, 7)], recv_sems.at[0])
 
     def put_shown(x):
-        shown_out[...] = x.reshape(8, 64, 128)
+        for p in range(4):
+            shown_out[:, p, :] = x[64 * p:64 * (p + 1)]
 
     for load in loads[2:10]:
         load.wait()
     owner_forward(cams, pick, image_of, par3, shown3, put_shown)
-    to_img(lambda t: shown_out.at[t], shown_mid.at[i], 1)
+    to_dev(shown_out, shown_mid, 1)
     for load in loads[10:]:
         load.wait()
     renderer_tables(lists_ref, order_ref, where_ref, live_ref, target_ref, listed, sort, place, tri, wanted)
-    landed(shown_mid.at[pl.ds(0, 7)], recv_sems.at[1])
-    to_dev(shown_mid, shown_in, 2)
-    landed(shown_in.at[:, pl.ds(0, 63), :], recv_sems.at[2])
+    landed(shown_mid.at[pl.ds(0, 63)], recv_sems.at[1])
+    for p in range(4):
+        low_half, high_half = exchange_halves(shown_mid[0:32, p, :], shown_mid[32:64, p, :])
+        shown_send[p] = low_half
+        shown_send[p + 4] = high_half
+    to_img(lambda t: shown_send.at[t], shown_in.at[i], 2)
+    landed(shown_in.at[pl.ds(0, 7)], recv_sems.at[2])
 
     def put_back(x):
-        back_out[...] = x.reshape(8, 64, 128)
+        back_out[...] = x.reshape(8, 32, 128)
 
     render(
-        shown_in[...].reshape(512, 128),
+        shown_in[...].reshape(256, 128),
         listed, sort, place, tri, wanted, tile3, coef3, grad3, front3, alpha3, weight3, high3, low3,
         put_back,
     )
-    to_dev(back_out, back_mid, 3)
-    landed(back_mid.at[:, pl.ds(0, 63), :], recv_sems.at[3])
-    to_img(lambda t: back_mid.at[t], back_in.at[i], 4)
-    landed(back_in.at[pl.ds(0, 7)], recv_sems.at[4])
-    owner_gradient(back_in[...].reshape(512, 128), cams, pick, image_of, par3, shown3, owner3)
+    to_img(lambda t: back_out.at[t], back_mid.at[i], 3)
+    landed(back_mid.at[pl.ds(0, 7)], recv_sems.at[3])
+    for p in range(4):
+        low_half, high_half = exchange_halves(back_mid[p], back_mid[p + 4])
+        back_send[0:32, p, :] = low_half
+        back_send[32:64, p, :] = high_half
+    to_dev(back_send, back_in, 4)
+    landed(back_in.at[pl.ds(0, 63)], recv_sems.at[4])
+    got = jnp.concatenate([back_in[:, p, :] for p in range(4)], axis=0)
+    owner_gradient(got, cams, pick, image_of, par3, shown3, owner3)
     for g in range(8):
         out_ref[:, 256 * g:256 * (g + 1)] = owner3[:, g, :]
     landed(cams.at[pl.ds(0, 7)], send_sems.at[0])
-    landed(shown_out.at[pl.ds(0, 7)], send_sems.at[1])
-    landed(shown_mid.at[:, pl.ds(0, 63), :], send_sems.at[2])
-    landed(back_out.at[:, pl.ds(0, 63), :], send_sems.at[3])
-    landed(back_mid.at[pl.ds(0, 7)], send_sems.at[4])
+    landed(shown_out.at[pl.ds(0, 63)], send_sems.at[1])
+    landed(shown_send.at[pl.ds(0, 7)], send_sems.at[2])
+    landed(back_out.at[pl.ds(0, 7)], send_sems.at[3])
+    landed(back_send.at[pl.ds(0, 63)], send_sems.at[4])
 
 
 def local(
     params, first_moment, second_moment, send_blocks, tile_blocks, tile_live, depth_order, tile_where, target, camera
 ):
     vmem = pl.BlockSpec(memory_space=pltpu.VMEM)
-    whole = pl.BlockSpec(memory_space=pl.ANY)
+    whole = pl.BlockSpec(memory_space=pltpu.HBM)
     integer = jnp.int32
-    block = pltpu.VMEM((8, 64, 128), F32)
+    by_dev = pltpu.VMEM((64, 4, 128), F32)
+    by_img = pltpu.VMEM((8, 32, 128), F32)
+    operands = (
+        params,
+        send_blocks,
+        tile_blocks.reshape(1, 512),
+        depth_order.reshape(8, 256),
+        tile_where,
+        tile_live,
+        target.reshape(8, 768),
+        camera,
+    )
     gradient = pl.pallas_call(
         step,
         out_shape=jax.ShapeDtypeStruct((59, 2048), F32),
@@ -504,19 +537,11 @@
         + [pltpu.VMEM((59, 8, 256), F32)]
         + RENDER_SCRATCH
         + [pltpu.VMEM((8, 128), F32)] * 2
-        + [block] * 6
+        + [by_dev] * 4
+        + [by_img] * 4
         + [pltpu.SemaphoreType.DMA((5,)), pltpu.SemaphoreType.DMA((5,)), pltpu.SemaphoreType.DMA],
-        compiler_params=pltpu.CompilerParams(collective_id=0, has_side_effects=True, vmem_limit_bytes=56 << 20),
-    )(
-        params,
-        send_blocks,
-        tile_blocks.reshape(1, 512),
-        depth_order.reshape(8, 256),
-        tile_where,
-        tile_live,
-        target.reshape(8, 768),
-        camera,
-    )
+        compiler_params=pltpu.CompilerParams(collective_id=0, has_side_effects=True, vmem_limit_bytes=24 << 20),
+    )(*[pltpu.with_memory_space_constraint(operand, pltpu.HBM) for operand in operands])
     new_first = 0.9 * first_moment + 0.1 * gradient
     new_second = 0.999 * second_moment + 0.001 * gradient * gradient
     new_params = params - rate_column() * new_first / (jnp.sqrt(new_second) + 1e-15)

time: 63.3 us -> 55.8 us (0.88)
  Pallas kernels: 59.9 us -> 52.6 us
    pallas_call x1, Pallas kernels: 59.9 us -> 52.6 us  [local(): pl.pallas_call(step, out_shape=jax.ShapeDtypeStruct((59, 2048), F32), in_...]
where the time goes in v3:
time: 55.8 us; the launch traced here: 55.6 us
  Pallas kernels  52.6 us (94%)
  other arithmetic  2.36 us (4%)
  between operations  0.68 us (1%)
    pallas_call x1, Pallas kernels, local(): pl.pallas_call(step, out_shape=jax.ShapeDtypeStruct((59, 2048), F32), in_...  52.6 us
    sub x1, other arithmetic, local(): params - rate_column() * new_first / (jnp.sqrt(new_second) + 1e-15)  2.35 us

profile of v3, /device:TPU:1, one launch (start us, length us, event | category | flops | bytes accessed | tf_op | source)
XLA Modules:
  0.0 55.6 jit_solution(15964960203010002773)
XLA Ops:
  0.6 0.0 copy-start
  0.7 0.0 copy-start.1
  0.7 52.6 %shard_map.121 = f32[59,2048]{1,0:T(8,128)S(1)} custom-call(f32[59,2048]{1,0:T(8,128)} %params_hbm.1, s32[1,512]{1,0:T(1,128)} %send_hbm.1, s32[1,512]{1,0:T(1,128)} %bitcast.5, s32[8,256]{1,0:T(8,128)} %bitcast.4, s32[1,8]{1,0:T(1,128)} %where_hbm.1, s32[1,8]{1,0:T(1,128)} %live_hbm.1, f32[8,768]{1,0:T(8,128)} %bitcast.3, f32[1,12]{1,0:T(1,128)} %camera_hbm.1), custom_call_target="tpu_custom_call" | custom-call | tf_op jit(solution)/shard_map/pallas_call | solution.py:521
  53.2 0.0 copy-done
  53.2 0.0 copy-done.1
  53.2 2.4 %divide_subtract_fusion = (f32[59,2048]{1,0:T(8,128)}, f32[59,2048]{1,0:T(8,128)}, f32[59,2048]{1,0:T(8,128)}) fusion(f32[59,2048]{1,0:T(8,128)S(1)} %copy-done, f32[59]{0:T(128)S(1)} %compare_select_fusion.4, f32[59,2048]{1,0:T(8,128)S(1)} %shard_map.121, f32[59,2048]{1,0:T(8,128)S(1)} %copy-done.1, f32[59,2048]{1,0:T(8,128)} %param.12), kind=kLoop, calls=%fused_computation.2 | loop fusion | flops 1329152 | bytes 3383532 | tf_op jit(solution)/shard_map/sub | solution.py:547
  (1 shorter events, 0.0 us)
Async XLA Ops:
  0.6 52.6 %copy-start = (f32[59,2048]{1,0:T(8,128)S(1)}, f32[59,2048]{1,0:T(8,128)}, u32[]{:S(2)}) copy-start(f32[59,2048]{1,0:T(8,128)} %params_hbm.1) | copy-start | bytes 1449988
  0.7 52.6 %copy-start.1 = (f32[59,2048]{1,0:T(8,128)S(1)}, f32[59,2048]{1,0:T(8,128)}, u32[]{:S(2)}) copy-start(f32[59,2048]{1,0:T(8,128)} %param.11) | copy-start | bytes 1449988

commit v4 on v3

--- a/solution.py
+++ b/solution.py
@@ -156,6 +156,22 @@
         image_of[g:g + 1, :] = images[0:1, 256 * g:256 * (g + 1)]
 
 
+def as_column(row):
+    row = row.astype(F32)
+    row = jnp.concatenate([row, jnp.zeros((128 - row.shape[0], row.shape[1]), F32)], axis=0)
+    return jnp.transpose(row)
+
+
+def owner_tables_back(send_ref, pick_back):
+    send = as_column(send_ref[...])[:, 0:1].astype(jnp.int32)
+
+    def chunk(g, carry):
+        pick_back[g] = one_hot(iota((512, 256), 1) // 4 + g * 64 == send)
+        return carry
+
+    lax.fori_loop(0, 8, chunk, 0)
+
+
 def cameras_of(cam_ref, image_of):
     image = image_of[...]
     masks = [image == float(i) for i in range(8)]
@@ -186,11 +202,11 @@
     put(paired_rows(fold(total, 3)))
 
 
-def owner_gradient(got, cam_ref, pick, image_of, par3, shown3, grad3):
-    parts = jnp.concatenate(pieces(unpaired(got), 3), axis=0)
+def owner_gradient(got, cam_ref, pick_back, image_of, par3, shown3, grad3):
+    parts = jnp.concatenate(pieces(unpaired(got), 2), axis=0)
     within = iota((16, 256), 1) % 4
     for g in range(8):
-        spread = fold(nt(parts, pick[256 * g:256 * (g + 1), :]), 3)
+        spread = fold(nn(parts, pick_back[g]), 2)
         total = jnp.zeros((16, 256), F32)
         for b in range(4):
             total = total + jnp.where(within == b, spread[16 * b:16 * (b + 1)], 0.0)
@@ -203,7 +219,9 @@
         grad3[c] = grads[c]
 
 
-def renderer_tables(lists_ref, order_ref, where_ref, live_ref, target_ref, listed, sort, place, tri, wanted):
+def renderer_tables(
+    lists_ref, order_ref, where_ref, live_ref, target_ref, listed, sort, place, tri, wanted, listed_back, sort_back
+):
     spot = iota((512, 512), 0)
     listed[...] = one_hot(spot // 32 % 8 * 64 + spot // 256 * 32 + spot % 32 == lists_ref[...])
 
@@ -214,6 +232,13 @@
         return carry
 
     lax.fori_loop(0, 8, one_tile, 0)
+    spot = iota((512, 512), 1)
+    column = as_column(lists_ref[...])[:, 0:1].astype(jnp.int32)
+    listed_back[...] = one_hot(spot // 32 % 8 * 64 + spot // 256 * 32 + spot % 32 == column)
+    order = order_ref[...]
+    column = as_column((order % 4) * 128 + (iota((8, 256), 0) % 2) * 64 + order // 4)
+    for n in range(8):
+        sort_back[n] = one_hot(iota((256, 512), 1) == column[:, n:n + 1].astype(jnp.int32))
     lane = iota((8, 512), 1)
     tile = lane // 64
     where = jnp.zeros((8, 512), jnp.int32)
@@ -240,7 +265,9 @@
     return out.astype(BF16)
 
 
-def render(got, listed, sort, place, tri, wanted, tile3, coef3, grad3, front3, alpha3, weight3, high3, low3, put):
+def render(
+    got, listed, sort, place, tri, wanted, listed_back, sort_back, tile3, coef3, grad3, front3, alpha3, weight3, high3, low3, put
+):
     rows = unpaired(got)
     tiles = fold(nn(jnp.concatenate(pieces(rows, 3), axis=0), listed[...]), 3)
     for b in range(4):
@@ -314,7 +341,7 @@
         moments = [s0, s0 * column, s1, s0 * column * column, s1 * column, s2]
         back = jnp.concatenate([jnp.sum(m, axis=0, keepdims=True) for m in moments] + [zero8[0:2], front3[n]], axis=0)
         pair = slice(128 * (n // 2), 128 * (n // 2) + 128)
-        spread = fold(nt(jnp.concatenate(pieces(back, 3), axis=0), sort[n]), 3)
+        spread = fold(nn(jnp.concatenate(pieces(back, 3), axis=0), sort_back[n]), 3)
         for b in range(4):
             grad3[:, b, pair] += spread[:, 128 * b:128 * (b + 1)]
 
@@ -331,7 +358,7 @@
     for q in range(9, 16):
         tile3[q, 0:4] = jnp.zeros((4, 512), F32)
     rows = jnp.concatenate([tile3[:, b, :] for b in range(4)], axis=0)
-    put(paired_rows(fold(nt(jnp.concatenate(pieces(rows, 3), axis=0), listed[...]), 3)))
+    put(paired_rows(fold(nn(jnp.concatenate(pieces(rows, 2), axis=0), listed_back[...]), 2)))
 
 
 def rate_column():
@@ -359,6 +386,7 @@
     pltpu.VMEM((8, 256), F32),
     pltpu.VMEM((59, 8, 256), F32),
     pltpu.VMEM((16, 8, 256), F32),
+    pltpu.VMEM((8, 512, 256), BF16),
 ]
 RENDER_SCRATCH = [
     pltpu.VMEM((512, 512), BF16),
@@ -366,6 +394,8 @@
     pltpu.VMEM((3, 8, 512), F32),
     pltpu.VMEM((2, 256, 256), BF16),
     pltpu.VMEM((8, 256, 8), F32),
+    pltpu.VMEM((512, 512), BF16),
+    pltpu.VMEM((8, 256, 512), BF16),
     pltpu.VMEM((16, 8, 512), F32),
     pltpu.VMEM((16, 8, 512), F32),
     pltpu.VMEM((16, 8, 512), F32),
@@ -382,10 +412,11 @@
 
 
 def step(
-    params_hbm, send_hbm, lists_hbm, order_hbm, where_hbm, live_hbm, target_hbm, camera_hbm, out_ref,
+    params_hbm, send_hbm, lists_hbm, order_hbm, where_hbm, live_hbm, target_hbm, camera_hbm, first_hbm, second_hbm,
+    new_params, new_first, new_second,
     send_ref, lists_ref, order_ref, where_ref, live_ref, target_ref, camera_ref, in_sems,
-    pick, image_of, par3, shown3, owner3,
-    listed, sort, place, tri, wanted, tile3, coef3, grad3, front3, alpha3, weight3, high3, low3,
+    pick, image_of, par3, shown3, pick_back, owner3, params_ref, first_ref, second_ref,
+    listed, sort, place, tri, wanted, listed_back, sort_back, tile3, coef3, grad3, front3, alpha3, weight3, high3, low3,
     cam_row, cams, shown_out, shown_mid, back_send, back_in, shown_send, shown_in, back_out, back_mid, send_sems, recv_sems, own_sem,
 ):
     i = lax.axis_index("img")
@@ -406,7 +437,7 @@
             [(camera_hbm, camera_ref), (send_hbm, send_ref)]
             + [(params_hbm.at[:, pl.ds(256 * g, 256)], par3.at[:, g, :]) for g in range(8)]
             + [(lists_hbm, lists_ref), (order_hbm, order_ref), (where_hbm, where_ref), (live_hbm, live_ref)]
-            + [(target_hbm, target_ref)]
+            + [(target_hbm, target_ref), (params_hbm, params_ref), (first_hbm, first_ref), (second_hbm, second_ref)]
         )
     ]
     for load in loads:
@@ -464,13 +495,16 @@
     to_dev(shown_out, shown_mid, 1)
     for load in loads[10:]:
         load.wait()
-    renderer_tables(lists_ref, order_ref, where_ref, live_ref, target_ref, listed, sort, place, tri, wanted)
+    renderer_tables(
+        lists_ref, order_ref, where_ref, live_ref, target_ref, listed, sort, place, tri, wanted, listed_back, sort_back
+    )
     landed(shown_mid.at[pl.ds(0, 63)], recv_sems.at[1])
     for p in range(4):
         low_half, high_half = exchange_halves(shown_mid[0:32, p, :], shown_mid[32:64, p, :])
         shown_send[p] = low_half
         shown_send[p + 4] = high_half
     to_img(lambda t: shown_send.at[t], shown_in.at[i], 2)
+    owner_tables_back(send_ref, pick_back)
     landed(shown_in.at[pl.ds(0, 7)], recv_sems.at[2])
 
     def put_back(x):
@@ -478,7 +512,7 @@
 
     render(
         shown_in[...].reshape(256, 128),
-        listed, sort, place, tri, wanted, tile3, coef3, grad3, front3, alpha3, weight3, high3, low3,
+        listed, sort, place, tri, wanted, listed_back, sort_back, tile3, coef3, grad3, front3, alpha3, weight3, high3, low3,
         put_back,
     )
     to_img(lambda t: back_out.at[t], back_mid.at[i], 3)
@@ -490,14 +524,21 @@
     to_dev(back_send, back_in, 4)
     landed(back_in.at[pl.ds(0, 63)], recv_sems.at[4])
     got = jnp.concatenate([back_in[:, p, :] for p in range(4)], axis=0)
-    owner_gradient(got, cams, pick, image_of, par3, shown3, owner3)
-    for g in range(8):
-        out_ref[:, 256 * g:256 * (g + 1)] = owner3[:, g, :]
+    owner_gradient(got, cams, pick_back, image_of, par3, shown3, owner3)
+    adam(owner3, params_ref, first_ref, second_ref, new_params, new_first, new_second)
     landed(cams.at[pl.ds(0, 7)], send_sems.at[0])
     landed(shown_out.at[pl.ds(0, 63)], send_sems.at[1])
     landed(shown_send.at[pl.ds(0, 7)], send_sems.at[2])
     landed(back_out.at[pl.ds(0, 7)], send_sems.at[3])
     landed(back_send.at[pl.ds(0, 63)], send_sems.at[4])
+
+
+def write_out(*refs):
+    copies = [pltpu.make_async_copy(refs[c], refs[3 + c], refs[6].at[c]) for c in range(3)]
+    for copy in copies:
+        copy.start()
+    for copy in copies:
+        copy.wait()
 
 
 def local(
@@ -517,12 +558,15 @@
         tile_live,
         target.reshape(8, 768),
         camera,
+        first_moment,
+        second_moment,
     )
-    gradient = pl.pallas_call(
+    shape = jax.ShapeDtypeStruct((59, 2048), F32)
+    updated = pl.pallas_call(
         step,
-        out_shape=jax.ShapeDtypeStruct((59, 2048), F32),
-        in_specs=[whole] * 8,
-        out_specs=vmem,
+        out_shape=(shape, shape, shape),
+        in_specs=[whole] * 10,
+        out_specs=(vmem, vmem, vmem),
         scratch_shapes=[
             pltpu.VMEM((1, 512), integer),
             pltpu.VMEM((1, 512), integer),
@@ -531,21 +575,25 @@
             pltpu.VMEM((1, 8), integer),
             pltpu.VMEM((8, 768), F32),
             pltpu.VMEM((1, 12), F32),
-            pltpu.SemaphoreType.DMA((15,)),
+            pltpu.SemaphoreType.DMA((18,)),
         ]
         + OWNER_SCRATCH
         + [pltpu.VMEM((59, 8, 256), F32)]
+        + [pltpu.VMEM((59, 2048), F32)] * 3
         + RENDER_SCRATCH
         + [pltpu.VMEM((8, 128), F32)] * 2
         + [by_dev] * 4
         + [by_img] * 4
         + [pltpu.SemaphoreType.DMA((5,)), pltpu.SemaphoreType.DMA((5,)), pltpu.SemaphoreType.DMA],
-        compiler_params=pltpu.CompilerParams(collective_id=0, has_side_effects=True, vmem_limit_bytes=24 << 20),
+        compiler_params=pltpu.CompilerParams(collective_id=0, has_side_effects=True, vmem_limit_bytes=36 << 20),
     )(*[pltpu.with_memory_space_constraint(operand, pltpu.HBM) for operand in operands])
-    new_first = 0.9 * first_moment + 0.1 * gradient
-    new_second = 0.999 * second_moment + 0.001 * gradient * gradient
-    new_params = params - rate_column() * new_first / (jnp.sqrt(new_second) + 1e-15)
-    return new_params, new_first, new_second
+    return pl.pallas_call(
+        write_out,
+        out_shape=(shape, shape, shape),
+        in_specs=[vmem] * 3,
+        out_specs=(whole, whole, whole),
+        scratch_shapes=[pltpu.SemaphoreType.DMA((3,))],
+    )(*updated)
 
 
 def solution(mesh):

time: 55.8 us -> 58.4 us (1.047)
  Pallas kernels: 52.6 us -> 55.2 us
  local copies, waits for them, and re-layouts: 0.01 us -> 2.37 us
  other arithmetic: 2.36 us -> 0 us
    pallas_call x1 -> x2, Pallas kernels: 52.6 us -> 55.2 us  [the longest x1 52.7 us: local(): pl.pallas_call(step, out_shape=(shape, shape, shape), in_specs=[whole] *...]
    unnamed x4 -> x6, local copies, waits for them, and re-layouts: 0.01 us -> 2.37 us
    sub x1 -> x0, other arithmetic: 2.35 us -> none  [local(): params - rate_column() * new_first / (jnp.sqrt(new_second) + 1e-15)]
where the time goes in v4:
time: 58.4 us; the launch traced here: 58.2 us
  Pallas kernels  55.2 us (95%)
  local copies, waits for them, and re-layouts  2.37 us (4%)
  between operations  0.65 us (1%)
    pallas_call x1, Pallas kernels, local(): pl.pallas_call(step, out_shape=(shape, shape, shape), in_specs=[whole] *...  52.7 us
    pallas_call x1, Pallas kernels, local(): pl.pallas_call(write_out, out_shape=(shape, shape, shape), in_specs=[vmem...  2.52 us
    unnamed x6, local copies, waits for them, and re-layouts  2.37 us

profile of v4, /device:TPU:1, one launch (start us, length us, event | category | flops | bytes accessed | tf_op | source)
XLA Modules:
  0.0 58.2 jit_solution(2936224285088703820)
XLA Ops:
  0.6 52.7 %shard_map.121 = (f32[59,2048]{1,0:T(8,128)S(1)}, f32[59,2048]{1,0:T(8,128)S(1)}, f32[59,2048]{1,0:T(8,128)S(1)}) custom-call(f32[59,2048]{1,0:T(8,128)} %params_hbm.1, s32[1,512]{1,0:T(1,128)} %send_hbm.1, s32[1,512]{1,0:T(1,128)} %bitcast.5, s32[8,256]{1,0:T(8,128)} %bitcast.4, s32[1,8]{1,0:T(1,128)} %where_hbm.1, s32[1,8]{1,0:T(1,128)} %live_hbm.1, ...), custom_call_target="tpu_custom_call" | custom-call | tf_op jit(solution)/shard_map/pallas_call | solution.py:565
  53.3 0.0 copy-start
  53.3 0.8 %copy-done = f32[59,2048]{1,0:T(8,128)} copy-done((f32[59,2048]{1,0:T(8,128)}, f32[59,2048]{1,0:T(8,128)S(1)}, u32[]{:S(2)}) %copy-start) | copy-done | bytes 483352
  54.1 0.0 copy-start.1
  54.1 0.8 %copy-done.1 = f32[59,2048]{1,0:T(8,128)} copy-done((f32[59,2048]{1,0:T(8,128)}, f32[59,2048]{1,0:T(8,128)S(1)}, u32[]{:S(2)}) %copy-start.1) | copy-done | bytes 483352
  54.9 0.0 copy-start.2
  54.9 0.8 %copy-done.2 = f32[59,2048]{1,0:T(8,128)} copy-done((f32[59,2048]{1,0:T(8,128)}, f32[59,2048]{1,0:T(8,128)S(1)}, u32[]{:S(2)}) %copy-start.2) | copy-done | bytes 483352
  55.7 2.5 %shard_map.122 = (f32[59,2048]{1,0:T(8,128)}, f32[59,2048]{1,0:T(8,128)}, f32[59,2048]{1,0:T(8,128)}) custom-call(f32[59,2048]{1,0:T(8,128)} %copy-done, f32[59,2048]{1,0:T(8,128)} %copy-done.1, f32[59,2048]{1,0:T(8,128)} %copy-done.2), custom_call_target="tpu_custom_call" | custom-call | tf_op jit(solution)/shard_map/pallas_call | solution.py:590
Async XLA Ops:
  53.3 0.8 %copy-start = (f32[59,2048]{1,0:T(8,128)}, f32[59,2048]{1,0:T(8,128)S(1)}, u32[]{:S(2)}) copy-start(f32[59,2048]{1,0:T(8,128)S(1)} %get-tuple-element.6.refs_0_) | copy-start | bytes 1449988
  54.1 0.8 %copy-start.1 = (f32[59,2048]{1,0:T(8,128)}, f32[59,2048]{1,0:T(8,128)S(1)}, u32[]{:S(2)}) copy-start(f32[59,2048]{1,0:T(8,128)S(1)} %get-tuple-element.7.refs_1_) | copy-start | bytes 1449988
  54.9 0.8 %copy-start.2 = (f32[59,2048]{1,0:T(8,128)}, f32[59,2048]{1,0:T(8,128)S(1)}, u32[]{:S(2)}) copy-start(f32[59,2048]{1,0:T(8,128)S(1)} %get-tuple-element.8.refs_2_) | copy-start | bytes 1449988

commit v5 on v4

--- a/solution.py
+++ b/solution.py
@@ -369,16 +369,23 @@
     return rate
 
 
-def adam(grad3, params_ref, first_ref, second_ref, new_params, new_first, new_second):
+def adam(both_ref, params_ref, first_ref, out_params, out_first, out_second, held_p, held_f, held_s, sems):
     rate = rate_column()
-    for g in range(8):
-        at = slice(256 * g, 256 * (g + 1))
-        gradient = grad3[:, g, :]
-        first = 0.9 * first_ref[:, at] + 0.1 * gradient
-        second = 0.999 * second_ref[:, at] + 0.001 * gradient * gradient
-        new_first[:, at] = first
-        new_second[:, at] = second
-        new_params[:, at] = params_ref[:, at] - rate * first / (jnp.sqrt(second) + 1e-15)
+    copies = []
+    for c in range(8):
+        at = slice(8 * c, min(8 * c + 8, 59))
+        gradient = both_ref[0, at, :]
+        first = 0.9 * first_ref[at, :] + 0.1 * gradient
+        second = 0.999 * both_ref[1, at, :] + 0.001 * gradient * gradient
+        held_f[at, :] = first
+        held_s[at, :] = second
+        held_p[at, :] = params_ref[at, :] - rate[at] * first / (jnp.sqrt(second) + 1e-15)
+        for part, (held, out) in enumerate(((held_p, out_params), (held_f, out_first), (held_s, out_second))):
+            copy = pltpu.make_async_copy(held.at[at, :], out.at[at, :], sems.at[3 * c + part])
+            copy.start()
+            copies.append(copy)
+    for copy in copies:
+        copy.wait()
 
 
 OWNER_SCRATCH = [
@@ -412,10 +419,9 @@
 
 
 def step(
-    params_hbm, send_hbm, lists_hbm, order_hbm, where_hbm, live_hbm, target_hbm, camera_hbm, first_hbm, second_hbm,
-    new_params, new_first, new_second,
+    params_hbm, send_hbm, lists_hbm, order_hbm, where_hbm, live_hbm, target_hbm, camera_hbm, second_hbm, out_ref,
     send_ref, lists_ref, order_ref, where_ref, live_ref, target_ref, camera_ref, in_sems,
-    pick, image_of, par3, shown3, pick_back, owner3, params_ref, first_ref, second_ref,
+    pick, image_of, par3, shown3, pick_back, owner3,
     listed, sort, place, tri, wanted, listed_back, sort_back, tile3, coef3, grad3, front3, alpha3, weight3, high3, low3,
     cam_row, cams, shown_out, shown_mid, back_send, back_in, shown_send, shown_in, back_out, back_mid, send_sems, recv_sems, own_sem,
 ):
@@ -437,7 +443,7 @@
             [(camera_hbm, camera_ref), (send_hbm, send_ref)]
             + [(params_hbm.at[:, pl.ds(256 * g, 256)], par3.at[:, g, :]) for g in range(8)]
             + [(lists_hbm, lists_ref), (order_hbm, order_ref), (where_hbm, where_ref), (live_hbm, live_ref)]
-            + [(target_hbm, target_ref), (params_hbm, params_ref), (first_hbm, first_ref), (second_hbm, second_ref)]
+            + [(target_hbm, target_ref), (second_hbm, out_ref.at[1])]
         )
     ]
     for load in loads:
@@ -525,20 +531,13 @@
     landed(back_in.at[pl.ds(0, 63)], recv_sems.at[4])
     got = jnp.concatenate([back_in[:, p, :] for p in range(4)], axis=0)
     owner_gradient(got, cams, pick_back, image_of, par3, shown3, owner3)
-    adam(owner3, params_ref, first_ref, second_ref, new_params, new_first, new_second)
+    for g in range(8):
+        out_ref[0, :, 256 * g:256 * (g + 1)] = owner3[:, g, :]
     landed(cams.at[pl.ds(0, 7)], send_sems.at[0])
     landed(shown_out.at[pl.ds(0, 63)], send_sems.at[1])
     landed(shown_send.at[pl.ds(0, 7)], send_sems.at[2])
     landed(back_out.at[pl.ds(0, 7)], send_sems.at[3])
     landed(back_send.at[pl.ds(0, 63)], send_sems.at[4])
-
-
-def write_out(*refs):
-    copies = [pltpu.make_async_copy(refs[c], refs[3 + c], refs[6].at[c]) for c in range(3)]
-    for copy in copies:
-        copy.start()
-    for copy in copies:
-        copy.wait()
 
 
 def local(
@@ -558,15 +557,14 @@
         tile_live,
         target.reshape(8, 768),
         camera,
-        first_moment,
         second_moment,
     )
     shape = jax.ShapeDtypeStruct((59, 2048), F32)
-    updated = pl.pallas_call(
+    gradient_second = pl.pallas_call(
         step,
-        out_shape=(shape, shape, shape),
-        in_specs=[whole] * 10,
-        out_specs=(vmem, vmem, vmem),
+        out_shape=jax.ShapeDtypeStruct((2, 59, 2048), F32),
+        in_specs=[whole] * 9,
+        out_specs=vmem,
         scratch_shapes=[
             pltpu.VMEM((1, 512), integer),
             pltpu.VMEM((1, 512), integer),
@@ -575,25 +573,25 @@
             pltpu.VMEM((1, 8), integer),
             pltpu.VMEM((8, 768), F32),
             pltpu.VMEM((1, 12), F32),
-            pltpu.SemaphoreType.DMA((18,)),
+            pltpu.SemaphoreType.DMA((16,)),
         ]
         + OWNER_SCRATCH
         + [pltpu.VMEM((59, 8, 256), F32)]
-        + [pltpu.VMEM((59, 2048), F32)] * 3
         + RENDER_SCRATCH
         + [pltpu.VMEM((8, 128), F32)] * 2
         + [by_dev] * 4
         + [by_img] * 4
         + [pltpu.SemaphoreType.DMA((5,)), pltpu.SemaphoreType.DMA((5,)), pltpu.SemaphoreType.DMA],
-        compiler_params=pltpu.CompilerParams(collective_id=0, has_side_effects=True, vmem_limit_bytes=36 << 20),
+        compiler_params=pltpu.CompilerParams(collective_id=0, has_side_effects=True, vmem_limit_bytes=24 << 20),
     )(*[pltpu.with_memory_space_constraint(operand, pltpu.HBM) for operand in operands])
     return pl.pallas_call(
-        write_out,
+        adam,
         out_shape=(shape, shape, shape),
         in_specs=[vmem] * 3,
         out_specs=(whole, whole, whole),
-        scratch_shapes=[pltpu.SemaphoreType.DMA((3,))],
-    )(*updated)
+        scratch_shapes=[pltpu.VMEM((59, 2048), F32)] * 3 + [pltpu.SemaphoreType.DMA((24,))],
+        compiler_params=pltpu.CompilerParams(vmem_limit_bytes=16 << 20),
+    )(gradient_second, params, first_moment)
 
 
 def solution(mesh):

time: 58.4 us -> 54.1 us (0.926)
  local copies, waits for them, and re-layouts: 2.37 us -> 0.01 us
  Pallas kernels: 55.2 us -> 53.3 us
    unnamed x6 -> x4, local copies, waits for them, and re-layouts: 2.37 us -> 0.01 us
    pallas_call x2, Pallas kernels: 55.2 us -> 53.3 us  [the longest x1 51.9 us: local(): pl.pallas_call(step, out_shape=jax.ShapeDtypeStruct((2, 59, 2048), F32),...]
where the time goes in v5:
time: 54.1 us; the launch traced here: 53.9 us
  Pallas kernels  53.3 us (99%)
  between operations  0.67 us (1%)
    pallas_call x1, Pallas kernels, local(): pl.pallas_call(step, out_shape=jax.ShapeDtypeStruct((2, 59, 2048), F32),...  51.9 us
    pallas_call x1, Pallas kernels, local(): pl.pallas_call(adam, out_shape=(shape, shape, shape), in_specs=[vmem] * 3...  1.38 us

profile of v5, /device:TPU:1, one launch (start us, length us, event | category | flops | bytes accessed | tf_op | source)
XLA Modules:
  0.0 53.9 jit_solution(101179502996031087)
XLA Ops:
  0.6 0.0 copy-start
  0.6 0.0 copy-start.1
  0.7 51.9 %shard_map.121.both_ref = f32[2,59,2048]{2,1,0:T(8,128)S(1)} custom-call(f32[59,2048]{1,0:T(8,128)} %params_ref.1, s32[1,512]{1,0:T(1,128)} %send_hbm.1, s32[1,512]{1,0:T(1,128)} %bitcast.5, s32[8,256]{1,0:T(8,128)} %bitcast.4, s32[1,8]{1,0:T(1,128)} %where_hbm.1, s32[1,8]{1,0:T(1,128)} %live_hbm.1, f32[8,768]{1,0:T(8,128)} %bitcast.3, f32[1,12]{1,0:T(1,128)} %camera_hbm.1, ...), custom_call_target="tpu_custom_call" | custom-call | tf_op jit(solution)/shard_map/pallas_call | solution.py:563
  52.5 0.0 copy-done
  52.5 0.0 copy-done.1
  52.5 1.4 %shard_map.122 = (f32[59,2048]{1,0:T(8,128)}, f32[59,2048]{1,0:T(8,128)}, f32[59,2048]{1,0:T(8,128)}) custom-call(f32[2,59,2048]{2,1,0:T(8,128)S(1)} %shard_map.121.both_ref, f32[59,2048]{1,0:T(8,128)S(1)} %copy-done, f32[59,2048]{1,0:T(8,128)S(1)} %copy-done.1), custom_call_target="tpu_custom_call" | custom-call | tf_op jit(solution)/shard_map/pallas_call | solution.py:587
Async XLA Ops:
  0.6 51.9 %copy-start = (f32[59,2048]{1,0:T(8,128)S(1)}, f32[59,2048]{1,0:T(8,128)}, u32[]{:S(2)}) copy-start(f32[59,2048]{1,0:T(8,128)} %params_ref.1) | copy-start | bytes 1449988
  0.6 51.9 %copy-start.1 = (f32[59,2048]{1,0:T(8,128)S(1)}, f32[59,2048]{1,0:T(8,128)}, u32[]{:S(2)}) copy-start(f32[59,2048]{1,0:T(8,128)} %first_ref.1) | copy-start | bytes 1449988

commit v6 on v5

--- a/solution.py
+++ b/solution.py
@@ -141,19 +141,14 @@
     return total
 
 
-def owner_tables(send_ref, pick, image_of):
-    send = send_ref[...]
-
-    def chunk(g, carry):
-        lanes = pl.ds(pl.multiple_of(g * 256, 256), 256)
-        pick[lanes, :] = one_hot(iota((256, 512), 0) // 4 + g * 64 == send)
-        return carry
-
-    lax.fori_loop(0, 8, chunk, 0)
-    image_row = jnp.broadcast_to((iota((8, 512), 1) // 64).astype(F32), (8, 512)).astype(BF16)
-    images = nt(image_row, pick[...])
-    for g in range(8):
-        image_of[g:g + 1, :] = images[0:1, 256 * g:256 * (g + 1)]
+def owner_tables(send_ref, pick, image_of, weave):
+    pick[...] = one_hot(iota((512, 512), 0) == send_ref[...])
+    row, column = iota((256, 256), 0), iota((256, 256), 1)
+    weave[0] = one_hot(row == column % 64 * 4 + column // 64)
+    weave[1] = one_hot(column == row % 64 * 4 + row // 64)
+    images = nt((iota((8, 512), 1) // 64).astype(F32).astype(BF16), pick[...])
+    own = jnp.where(iota((8, 512), 1) // 64 == iota((8, 512), 0), images, 0.0).astype(BF16)
+    image_of[...] = nn(own, one_hot(iota((512, 256), 0) % 64 == iota((512, 256), 1) // 4))
 
 
 def as_column(row):
@@ -163,13 +158,7 @@
 
 
 def owner_tables_back(send_ref, pick_back):
-    send = as_column(send_ref[...])[:, 0:1].astype(jnp.int32)
-
-    def chunk(g, carry):
-        pick_back[g] = one_hot(iota((512, 256), 1) // 4 + g * 64 == send)
-        return carry
-
-    lax.fori_loop(0, 8, chunk, 0)
+    pick_back[...] = one_hot(iota((512, 512), 1) == as_column(send_ref[...])[:, 0:1].astype(jnp.int32))
 
 
 def cameras_of(cam_ref, image_of):
@@ -185,42 +174,49 @@
     return out
 
 
-def owner_forward(cam_ref, pick, image_of, par3, shown3, put):
+def owner_forward(cam_ref, pick, image_of, weave, par3, shown3, put):
     shown = project([par3[c] for c in range(59)], cameras_of(cam_ref, image_of))
     for q in range(9):
         shown3[q] = shown[q]
     for q in range(9, 16):
         shown3[q] = jnp.zeros((8, 256), F32)
-    within = iota((16, 256), 1) % 4
-    total = jnp.zeros((192, 512), F32)
-    for g in range(8):
-        rows = []
-        for b in range(4):
-            rows.append(jnp.where(within == b, shown3[:, g, :], 0.0))
-        rows = jnp.concatenate(rows, axis=0)
-        total = total + nn(jnp.concatenate(pieces(rows, 3), axis=0), pick[256 * g:256 * (g + 1), :])
-    put(paired_rows(fold(total, 3)))
-
-
-def owner_gradient(got, cam_ref, pick_back, image_of, par3, shown3, grad3):
-    parts = jnp.concatenate(pieces(unpaired(got), 2), axis=0)
-    within = iota((16, 256), 1) % 4
-    for g in range(8):
-        spread = fold(nn(parts, pick_back[g]), 2)
-        total = jnp.zeros((16, 256), F32)
-        for b in range(4):
-            total = total + jnp.where(within == b, spread[16 * b:16 * (b + 1)], 0.0)
-        shown3[:, g, :] = total
-    values = [par3[c] for c in range(59)]
+    flat = shown3[0:10].reshape(80, 256)
+    shown3[0:10] = fold(nn(jnp.concatenate(pieces(flat, 3), axis=0), weave[0]), 3).reshape(10, 8, 256)
+    rows = [[], [], [], []]
+    for p in range(2):
+        at = slice(128 * p, 128 * (p + 1))
+        for t in range(4):
+            even, odd = exchange_halves(shown3[:, 2 * t, at], shown3[:, 2 * t + 1, at])
+            rows[2 * p].append(even)
+            rows[2 * p + 1].append(odd)
+    rows = jnp.concatenate([jnp.concatenate(row, axis=1) for row in rows], axis=0)
+    put(paired_rows(fold(nn(jnp.concatenate(pieces(rows, 3), axis=0), pick[...]), 3)))
+
+
+def owner_pullback(cam_ref, image_of, par3):
     cams = cameras_of(cam_ref, image_of)
-    _, pullback = jax.vjp(lambda v: project(v, cams), values)
-    (grads,) = pullback([shown3[q] for q in range(9)])
+    return jax.vjp(lambda v: project(v, cams), [par3[c] for c in range(59)])[1]
+
+
+def owner_gradient(got, pullback, pick_back, weave, shown3, grad3):
+    spread = fold(nn(jnp.concatenate(pieces(unpaired(got), 2), axis=0), pick_back[...]), 2)
+    for p in range(2):
+        at = slice(128 * p, 128 * (p + 1))
+        for t in range(4):
+            lanes = slice(128 * t, 128 * (t + 1))
+            even, odd = exchange_halves(spread[32 * p:32 * p + 16, lanes], spread[32 * p + 16:32 * p + 32, lanes])
+            shown3[:, 2 * t, at] = even
+            shown3[:, 2 * t + 1, at] = odd
+    flat = shown3[0:10].reshape(80, 256)
+    slopes = fold(nn(jnp.concatenate(pieces(flat, 2), axis=0), weave[1]), 2).reshape(10, 8, 256)
+    (grads,) = pullback([slopes[q] for q in range(9)])
     for c in range(59):
         grad3[c] = grads[c]
 
 
 def renderer_tables(
-    lists_ref, order_ref, where_ref, live_ref, target_ref, listed, sort, place, tri, wanted, listed_back, sort_back
+    lists_ref, order_ref, where_ref, live_ref, target_ref, listed, sort, place, tri, wanted, listed_back, sort_back, power,
+    tile3, coef3, grad3,
 ):
     spot = iota((512, 512), 0)
     listed[...] = one_hot(spot // 32 % 8 * 64 + spot // 256 * 32 + spot % 32 == lists_ref[...])
@@ -249,11 +245,14 @@
     place[0] = (where % 32 * 16 + 8).astype(F32)
     place[1] = (where // 32 * 16 + 8).astype(F32)
     place[2] = jnp.where(lane % 64 < live, 1.0, 0.0)
-    tri[0] = one_hot(iota((256, 256), 0) < iota((256, 256), 1))
-    tri[1] = one_hot(iota((256, 256), 0) > iota((256, 256), 1))
+    tri[0] = one_hot(iota((512, 256), 0) % 256 < iota((512, 256), 1))
+    tri[1] = one_hot(iota((512, 256), 0) % 256 > iota((512, 256), 1))
     for n in range(8):
         rows = [target_ref[n:n + 1, 256 * ch:256 * (ch + 1)] for ch in range(3)]
         wanted[n] = jnp.transpose(jnp.concatenate(rows + [jnp.zeros((125, 256), F32)], axis=0))[:, 0:8]
+    power[...] = monomials(iota((256, 48), 0), iota((256, 48), 1) % 16)
+    for held in (tile3, coef3, grad3):
+        held[...] = jnp.zeros(held.shape, F32)
 
 
 def monomials(pixel, term):
@@ -266,7 +265,7 @@
 
 
 def render(
-    got, listed, sort, place, tri, wanted, listed_back, sort_back, tile3, coef3, grad3, front3, alpha3, weight3, high3, low3, put
+    got, listed, sort, place, tri, wanted, listed_back, sort_back, power, tile3, coef3, grad3, front3, alpha3, weight3, split3, put
 ):
     rows = unpaired(got)
     tiles = fold(nn(jnp.concatenate(pieces(rows, 3), axis=0), listed[...]), 3)
@@ -291,10 +290,6 @@
     ] + [tile3[q, 0:4] for q in range(6, 9)]
     for c in range(9):
         coef3[c, 0:4] = coefs[c]
-    for c in range(9, 16):
-        coef3[c, 0:4] = jnp.zeros((4, 512), F32)
-    grad3[...] = jnp.zeros(grad3.shape, F32)
-    power = monomials(iota((256, 48), 0), iota((256, 48), 1) % 16)
     column = iota((16, 256), 0).astype(F32) - 7.5
     zero8 = jnp.zeros((8, 256), F32)
 
@@ -304,17 +299,17 @@
         sorted_parts = nn(jnp.concatenate(pieces(mine, 3), axis=0), sort[n])
         front = fold(sorted_parts, 3)
         front3[n] = jnp.where(iota((8, 256), 0) < 3, pltpu.roll(front, 10, 0)[0:8], 0.0)
-        alpha = jnp.exp2(nn(power, sorted_parts.astype(BF16)))
+        alpha = jnp.exp2(nn(power[...], sorted_parts.astype(BF16)))
         alpha3[n] = alpha
-        high3[n], low3[n] = pieces(jnp.log(1.0 - alpha), 2)
+        split3[n] = jnp.concatenate(pieces(jnp.log(1.0 - alpha), 2), axis=1)
     for n in range(8):
-        weight = jnp.exp(nn(high3[n], tri[0]) + nn(low3[n], tri[0])) * alpha3[n]
+        weight = jnp.exp(nn(split3[n], tri[0])) * alpha3[n]
         weight3[n] = weight
-        high3[n], low3[n] = pieces(weight, 2)
+        split3[n] = jnp.concatenate(pieces(weight, 2), axis=1)
     for n in range(8):
         colour = front3[n]
         c_all = jnp.concatenate(pieces(colour, 2), axis=0)
-        both = nt(high3[n], c_all) + nt(low3[n], c_all)
+        both = nt(split3[n], jnp.concatenate([c_all, c_all], axis=1))
         residual = both[:, 0:8] + both[:, 8:16] - wanted[n]
         weight = weight3[n]
         gain = jnp.zeros((256, 256), F32)
@@ -324,14 +319,14 @@
             shades.append(jnp.sum(residual[:, ch:ch + 1] * weight, axis=0, keepdims=True))
         passed = weight * gain
         weight3[n] = passed
-        high3[n], low3[n] = pieces(passed, 2)
+        split3[n] = jnp.concatenate(pieces(passed, 2), axis=1)
         front3[n] = jnp.concatenate(shades + [zero8[0:5]], axis=0)
     for n in range(8):
         alpha = alpha3[n]
         keep = 1.0 - alpha
         guess = pl.reciprocal(keep, approx=True)
         inverse = guess * (2.0 - keep * guess)
-        behind = nn(high3[n], tri[1]) + nn(low3[n], tri[1])
+        behind = nn(split3[n], tri[1])
         change = (weight3[n] - behind * (alpha * inverse)).reshape(16, 16, 256)
         s0, s1, s2 = change[0], -7.5 * change[0], 56.25 * change[0]
         for y in range(1, 16):
@@ -389,28 +384,29 @@
 
 
 OWNER_SCRATCH = [
-    pltpu.VMEM((2048, 512), BF16),
+    pltpu.VMEM((512, 512), BF16),
     pltpu.VMEM((8, 256), F32),
+    pltpu.VMEM((2, 256, 256), BF16),
     pltpu.VMEM((59, 8, 256), F32),
     pltpu.VMEM((16, 8, 256), F32),
-    pltpu.VMEM((8, 512, 256), BF16),
+    pltpu.VMEM((512, 512), BF16),
 ]
 RENDER_SCRATCH = [
     pltpu.VMEM((512, 512), BF16),
     pltpu.VMEM((8, 512, 256), BF16),
     pltpu.VMEM((3, 8, 512), F32),
-    pltpu.VMEM((2, 256, 256), BF16),
+    pltpu.VMEM((2, 512, 256), BF16),
     pltpu.VMEM((8, 256, 8), F32),
     pltpu.VMEM((512, 512), BF16),
     pltpu.VMEM((8, 256, 512), BF16),
+    pltpu.VMEM((256, 48), BF16),
     pltpu.VMEM((16, 8, 512), F32),
     pltpu.VMEM((16, 8, 512), F32),
     pltpu.VMEM((16, 8, 512), F32),
     pltpu.VMEM((8, 8, 256), F32),
     pltpu.VMEM((8, 256, 256), F32),
     pltpu.VMEM((8, 256, 256), F32),
-    pltpu.VMEM((8, 256, 256), BF16),
-    pltpu.VMEM((8, 256, 256), BF16),
+    pltpu.VMEM((8, 256, 512), BF16),
 ]
 
 
@@ -421,8 +417,8 @@
 def step(
     params_hbm, send_hbm, lists_hbm, order_hbm, where_hbm, live_hbm, target_hbm, camera_hbm, second_hbm, out_ref,
     send_ref, lists_ref, order_ref, where_ref, live_ref, target_ref, camera_ref, in_sems,
-    pick, image_of, par3, shown3, pick_back, owner3,
-    listed, sort, place, tri, wanted, listed_back, sort_back, tile3, coef3, grad3, front3, alpha3, weight3, high3, low3,
+    pick, image_of, weave, par3, shown3, pick_back, owner3,
+    listed, sort, place, tri, wanted, listed_back, sort_back, power, tile3, coef3, grad3, front3, alpha3, weight3, split3,
     cam_row, cams, shown_out, shown_mid, back_send, back_in, shown_send, shown_in, back_out, back_mid, send_sems, recv_sems, own_sem,
 ):
     i = lax.axis_index("img")
@@ -454,7 +450,7 @@
     pl.semaphore_wait(barrier, 70)
 
     def to_img(source, target, phase):
-        for s in range(1, 8):
+        for s in (4, 3, 5, 2, 6, 1, 7):
             t = lax.rem(i + s, 8)
             pltpu.make_async_remote_copy(
                 src_ref=source(t),
@@ -488,7 +484,7 @@
 
     to_img(lambda t: cam_row.at[pl.ds(0, 1)], cams.at[pl.ds(i, 1)], 0)
     loads[1].wait()
-    owner_tables(send_ref, pick, image_of)
+    owner_tables(send_ref, pick, image_of, weave)
     landed(cams.at[pl.ds(0, 7)], recv_sems.at[0])
 
     def put_shown(x):
@@ -497,12 +493,13 @@
 
     for load in loads[2:10]:
         load.wait()
-    owner_forward(cams, pick, image_of, par3, shown3, put_shown)
+    owner_forward(cams, pick, image_of, weave, par3, shown3, put_shown)
     to_dev(shown_out, shown_mid, 1)
     for load in loads[10:]:
         load.wait()
     renderer_tables(
-        lists_ref, order_ref, where_ref, live_ref, target_ref, listed, sort, place, tri, wanted, listed_back, sort_back
+        lists_ref, order_ref, where_ref, live_ref, target_ref,
+        listed, sort, place, tri, wanted, listed_back, sort_back, power, tile3, coef3, grad3,
     )
     landed(shown_mid.at[pl.ds(0, 63)], recv_sems.at[1])
     for p in range(4):
@@ -518,7 +515,7 @@
 
     render(
         shown_in[...].reshape(256, 128),
-        listed, sort, place, tri, wanted, listed_back, sort_back, tile3, coef3, grad3, front3, alpha3, weight3, high3, low3,
+        listed, sort, place, tri, wanted, listed_back, sort_back, power, tile3, coef3, grad3, front3, alpha3, weight3, split3,
         put_back,
     )
     to_img(lambda t: back_out.at[t], back_mid.at[i], 3)
@@ -528,9 +525,10 @@
         back_send[0:32, p, :] = low_half
         back_send[32:64, p, :] = high_half
     to_dev(back_send, back_in, 4)
+    pullback = owner_pullback(cams, image_of, par3)
     landed(back_in.at[pl.ds(0, 63)], recv_sems.at[4])
     got = jnp.concatenate([back_in[:, p, :] for p in range(4)], axis=0)
-    owner_gradient(got, cams, pick_back, image_of, par3, shown3, owner3)
+    owner_gradient(got, pullback, pick_back, weave, shown3, owner3)
     for g in range(8):
         out_ref[0, :, 256 * g:256 * (g + 1)] = owner3[:, g, :]
     landed(cams.at[pl.ds(0, 7)], send_sems.at[0])

time: 54.1 us -> 53.6 us (level)
  no operation moved by 1% of the time
where the time goes in v6:
time: 53.6 us; the launch traced here: 53.5 us
  Pallas kernels  52.8 us (99%)
  between operations  0.67 us (1%)
    pallas_call x1, Pallas kernels, local(): pl.pallas_call(step, out_shape=jax.ShapeDtypeStruct((2, 59, 2048), F32),...  51.4 us
    pallas_call x1, Pallas kernels, local(): pl.pallas_call(adam, out_shape=(shape, shape, shape), in_specs=[vmem] * 3...  1.38 us

profile of v6, /device:TPU:1, one launch (start us, length us, event | category | flops | bytes accessed | tf_op | source)
XLA Modules:
  0.0 53.5 jit_solution(3696577040671175756)
XLA Ops:
  0.6 0.0 copy-start
  0.6 0.0 copy-start.1
  0.7 51.4 %shard_map.121.both_ref = f32[2,59,2048]{2,1,0:T(8,128)S(1)} custom-call(f32[59,2048]{1,0:T(8,128)} %params_ref.1, s32[1,512]{1,0:T(1,128)} %send_hbm.1, s32[1,512]{1,0:T(1,128)} %bitcast.5, s32[8,256]{1,0:T(8,128)} %bitcast.4, s32[1,8]{1,0:T(1,128)} %where_hbm.1, s32[1,8]{1,0:T(1,128)} %live_hbm.1, f32[8,768]{1,0:T(8,128)} %bitcast.3, f32[1,12]{1,0:T(1,128)} %camera_hbm.1, ...), custom_call_target="tpu_custom_call" | custom-call | tf_op jit(solution)/shard_map/pallas_call | solution.py:561
  52.0 0.0 copy-done
  52.1 0.0 copy-done.1
  52.1 1.4 %shard_map.122 = (f32[59,2048]{1,0:T(8,128)}, f32[59,2048]{1,0:T(8,128)}, f32[59,2048]{1,0:T(8,128)}) custom-call(f32[2,59,2048]{2,1,0:T(8,128)S(1)} %shard_map.121.both_ref, f32[59,2048]{1,0:T(8,128)S(1)} %copy-done, f32[59,2048]{1,0:T(8,128)S(1)} %copy-done.1), custom_call_target="tpu_custom_call" | custom-call | tf_op jit(solution)/shard_map/pallas_call | solution.py:585
Async XLA Ops:
  0.6 51.4 %copy-start = (f32[59,2048]{1,0:T(8,128)S(1)}, f32[59,2048]{1,0:T(8,128)}, u32[]{:S(2)}) copy-start(f32[59,2048]{1,0:T(8,128)} %params_ref.1) | copy-start | bytes 1449988
  0.6 51.4 %copy-start.1 = (f32[59,2048]{1,0:T(8,128)S(1)}, f32[59,2048]{1,0:T(8,128)}, u32[]{:S(2)}) copy-start(f32[59,2048]{1,0:T(8,128)} %first_ref.1) | copy-start | bytes 1449988

commit v7 on v6

--- a/solution.py
+++ b/solution.py
@@ -118,13 +118,38 @@
     return lax.dot_general(a, b, (((1,), (1,)), ((), ())), preferred_element_type=F32)
 
 
-def paired_rows(x):
-    return jnp.transpose(jnp.concatenate([x[:, 0:256], x[:, 256:512]], axis=0))
-
-
-def unpaired(x):
-    down = jnp.transpose(x)
-    return jnp.concatenate([down[0:64], down[64:128]], axis=1)
+def turned(x):
+    rows, columns = x.shape
+    side = -columns % 128
+    if side:
+        x = jnp.concatenate([x, jnp.zeros((rows, side), F32)], axis=1)
+    return jnp.transpose(x)[0:columns]
+
+
+def thirds(x):
+    return turned(jnp.concatenate(list(x) + [jnp.zeros((8, 192), F32)], axis=0))
+
+
+def by_image(x):
+    x = jnp.concatenate([x[16 * b:16 * b + 10] for b in range(4)], axis=0)
+    last = jnp.concatenate([x[:, 384:512], jnp.zeros((40, 64), F32)], axis=1)
+    return thirds([x[:, 0:192], x[:, 192:384], last])
+
+
+def from_images(x):
+    down = turned(x)
+    down = jnp.concatenate([down[0:40], down[40:80], down[80:120, 0:128]], axis=1)
+    rest = jnp.zeros((6, 512), F32)
+    return jnp.concatenate([part for b in range(4) for part in (down[10 * b:10 * b + 10], rest)], axis=0)
+
+
+def regroup(rows, count, kept):
+    lane = iota((count, 128), 1)
+    total = jnp.zeros((count, 128), F32)
+    for g, x in enumerate(rows):
+        moved = x if g == kept else pltpu.roll(x, 40 * (g - kept) % 128, 1)
+        total = jnp.where((lane >= 40 * g) & (lane < 40 * g + 40), moved, total)
+    return total
 
 
 def exchange_halves(a, b):
@@ -190,7 +215,7 @@
             rows[2 * p].append(even)
             rows[2 * p + 1].append(odd)
     rows = jnp.concatenate([jnp.concatenate(row, axis=1) for row in rows], axis=0)
-    put(paired_rows(fold(nn(jnp.concatenate(pieces(rows, 3), axis=0), pick[...]), 3)))
+    put(by_image(fold(nn(jnp.concatenate(pieces(rows, 3), axis=0), pick[...]), 3)))
 
 
 def owner_pullback(cam_ref, image_of, par3):
@@ -199,7 +224,7 @@
 
 
 def owner_gradient(got, pullback, pick_back, weave, shown3, grad3):
-    spread = fold(nn(jnp.concatenate(pieces(unpaired(got), 2), axis=0), pick_back[...]), 2)
+    spread = fold(nn(jnp.concatenate(pieces(from_images(got), 2), axis=0), pick_back[...]), 2)
     for p in range(2):
         at = slice(128 * p, 128 * (p + 1))
         for t in range(4):
@@ -218,8 +243,14 @@
     lists_ref, order_ref, where_ref, live_ref, target_ref, listed, sort, place, tri, wanted, listed_back, sort_back, power,
     tile3, coef3, grad3,
 ):
-    spot = iota((512, 512), 0)
-    listed[...] = one_hot(spot // 32 % 8 * 64 + spot // 256 * 32 + spot % 32 == lists_ref[...])
+    def owner_at(h, spot):
+        column = 24 * h + spot % 24
+        return jnp.where(column < 64, spot // 24 * 64 + column, -1)
+
+    column = as_column(lists_ref[...])[:, 0:1].astype(jnp.int32)
+    for h in range(3):
+        listed[h] = one_hot(owner_at(h, iota((192, 512), 0)) == lists_ref[...])
+        listed_back[h] = one_hot(owner_at(h, iota((512, 192), 1)) == column)
 
     def one_tile(n, carry):
         order = order_ref[pl.ds(n, 1), :]
@@ -228,9 +259,6 @@
         return carry
 
     lax.fori_loop(0, 8, one_tile, 0)
-    spot = iota((512, 512), 1)
-    column = as_column(lists_ref[...])[:, 0:1].astype(jnp.int32)
-    listed_back[...] = one_hot(spot // 32 % 8 * 64 + spot // 256 * 32 + spot % 32 == column)
     order = order_ref[...]
     column = as_column((order % 4) * 128 + (iota((8, 256), 0) % 2) * 64 + order // 4)
     for n in range(8):
@@ -267,10 +295,13 @@
 def render(
     got, listed, sort, place, tri, wanted, listed_back, sort_back, power, tile3, coef3, grad3, front3, alpha3, weight3, split3, put
 ):
-    rows = unpaired(got)
-    tiles = fold(nn(jnp.concatenate(pieces(rows, 3), axis=0), listed[...]), 3)
+    rows = turned(got)
+    tiles = jnp.zeros((48, 512), F32)
+    for h in range(3):
+        third = jnp.concatenate([rows[40 * h:40 * h + 40], jnp.zeros((8, 192), F32)], axis=0)
+        tiles = tiles + fold(nn(jnp.concatenate(pieces(third, 3), axis=0), listed[h]), 3)
     for b in range(4):
-        tile3[:, b, :] = tiles[16 * b:16 * (b + 1)]
+        tile3[0:10, b, :] = tiles[10 * b:10 * b + 10]
     centre_x, centre_y, live = place[0, 0:4], place[1, 0:4], place[2, 0:4]
 
     def geometry():
@@ -352,8 +383,9 @@
         tile3[q, 0:4] = results[q]
     for q in range(9, 16):
         tile3[q, 0:4] = jnp.zeros((4, 512), F32)
-    rows = jnp.concatenate([tile3[:, b, :] for b in range(4)], axis=0)
-    put(paired_rows(fold(nn(jnp.concatenate(pieces(rows, 2), axis=0), listed_back[...]), 2)))
+    rows = jnp.concatenate([tile3[0:10, b, :] for b in range(4)] + [jnp.zeros((8, 512), F32)], axis=0)
+    parts = jnp.concatenate(pieces(rows, 2), axis=0)
+    put(thirds([fold(nn(parts, listed_back[h]), 2)[0:40] for h in range(3)]))
 
 
 def rate_column():
@@ -392,12 +424,12 @@
     pltpu.VMEM((512, 512), BF16),
 ]
 RENDER_SCRATCH = [
-    pltpu.VMEM((512, 512), BF16),
+    pltpu.VMEM((3, 192, 512), BF16),
     pltpu.VMEM((8, 512, 256), BF16),
     pltpu.VMEM((3, 8, 512), F32),
     pltpu.VMEM((2, 512, 256), BF16),
     pltpu.VMEM((8, 256, 8), F32),
-    pltpu.VMEM((512, 512), BF16),
+    pltpu.VMEM((3, 512, 192), BF16),
     pltpu.VMEM((8, 256, 512), BF16),
     pltpu.VMEM((256, 48), BF16),
     pltpu.VMEM((16, 8, 512), F32),
@@ -488,8 +520,8 @@
     landed(cams.at[pl.ds(0, 7)], recv_sems.at[0])
 
     def put_shown(x):
-        for p in range(4):
-            shown_out[:, p, :] = x[64 * p:64 * (p + 1)]
+        for r in range(3):
+            shown_out[:, r, :] = x[64 * r:64 * (r + 1)]
 
     for load in loads[2:10]:
         load.wait()
@@ -502,32 +534,34 @@
         listed, sort, place, tri, wanted, listed_back, sort_back, power, tile3, coef3, grad3,
     )
     landed(shown_mid.at[pl.ds(0, 63)], recv_sems.at[1])
-    for p in range(4):
-        low_half, high_half = exchange_halves(shown_mid[0:32, p, :], shown_mid[32:64, p, :])
-        shown_send[p] = low_half
-        shown_send[p + 4] = high_half
+    for r in range(3):
+        rows = [shown_mid[0:24, r, :], shown_mid[24:48, r, :]]
+        rows.append(jnp.concatenate([shown_mid[48:64, r, :], jnp.zeros((8, 128), F32)], axis=0))
+        for g in range(3 if r < 2 else 2):
+            shown_send[3 * g + r] = regroup(rows, 24, g)
     to_img(lambda t: shown_send.at[t], shown_in.at[i], 2)
     owner_tables_back(send_ref, pick_back)
     landed(shown_in.at[pl.ds(0, 7)], recv_sems.at[2])
 
     def put_back(x):
-        back_out[...] = x.reshape(8, 32, 128)
+        back_out[...] = x.reshape(8, 24, 128)
 
     render(
-        shown_in[...].reshape(256, 128),
+        shown_in[...].reshape(192, 128),
         listed, sort, place, tri, wanted, listed_back, sort_back, power, tile3, coef3, grad3, front3, alpha3, weight3, split3,
         put_back,
     )
     to_img(lambda t: back_out.at[t], back_mid.at[i], 3)
     landed(back_mid.at[pl.ds(0, 7)], recv_sems.at[3])
-    for p in range(4):
-        low_half, high_half = exchange_halves(back_mid[p], back_mid[p + 4])
-        back_send[0:32, p, :] = low_half
-        back_send[32:64, p, :] = high_half
+    for r in range(3):
+        for h in range(3):
+            count = 24 if h < 2 else 16
+            rows = [back_mid[3 * g + r, 0:count, :] for g in range(3 if r < 2 else 2)]
+            back_send[24 * h:24 * h + count, r, :] = regroup(rows, count, h)
     to_dev(back_send, back_in, 4)
     pullback = owner_pullback(cams, image_of, par3)
     landed(back_in.at[pl.ds(0, 63)], recv_sems.at[4])
-    got = jnp.concatenate([back_in[:, p, :] for p in range(4)], axis=0)
+    got = jnp.concatenate([back_in[:, p, :] for p in range(3)], axis=0)
     owner_gradient(got, pullback, pick_back, weave, shown3, owner3)
     for g in range(8):
         out_ref[0, :, 256 * g:256 * (g + 1)] = owner3[:, g, :]
@@ -544,8 +578,8 @@
     vmem = pl.BlockSpec(memory_space=pltpu.VMEM)
     whole = pl.BlockSpec(memory_space=pltpu.HBM)
     integer = jnp.int32
-    by_dev = pltpu.VMEM((64, 4, 128), F32)
-    by_img = pltpu.VMEM((8, 32, 128), F32)
+    by_dev = pltpu.VMEM((64, 3, 128), F32)
+    by_img = pltpu.VMEM((8, 24, 128), F32)
     operands = (
         params,
         send_blocks,

time: 53.6 us -> 53.6 us (level)
  no operation moved by 1% of the time
where the time goes in v7:
time: 53.6 us; the launch traced here: 53.5 us
  Pallas kernels  52.8 us (99%)
  between operations  0.67 us (1%)
    pallas_call x1, Pallas kernels, local(): pl.pallas_call(step, out_shape=jax.ShapeDtypeStruct((2, 59, 2048), F32),...  51.4 us
    pallas_call x1, Pallas kernels, local(): pl.pallas_call(adam, out_shape=(shape, shape, shape), in_specs=[vmem] * 3...  1.38 us

profile of v7, /device:TPU:1, one launch (start us, length us, event | category | flops | bytes accessed | tf_op | source)
XLA Modules:
  0.0 53.5 jit_solution(7272262314889477105)
XLA Ops:
  0.6 0.0 copy-start
  0.6 0.0 copy-start.1
  0.7 51.4 %shard_map.121.both_ref = f32[2,59,2048]{2,1,0:T(8,128)S(1)} custom-call(f32[59,2048]{1,0:T(8,128)} %params_ref.1, s32[1,512]{1,0:T(1,128)} %send_hbm.1, s32[1,512]{1,0:T(1,128)} %bitcast.5, s32[8,256]{1,0:T(8,128)} %bitcast.4, s32[1,8]{1,0:T(1,128)} %where_hbm.1, s32[1,8]{1,0:T(1,128)} %live_hbm.1, f32[8,768]{1,0:T(8,128)} %bitcast.3, f32[1,12]{1,0:T(1,128)} %camera_hbm.1, ...), custom_call_target="tpu_custom_call" | custom-call | tf_op jit(solution)/shard_map/pallas_call | solution.py:595
  52.1 0.0 copy-done
  52.1 0.0 copy-done.1
  52.1 1.4 %shard_map.122 = (f32[59,2048]{1,0:T(8,128)}, f32[59,2048]{1,0:T(8,128)}, f32[59,2048]{1,0:T(8,128)}) custom-call(f32[2,59,2048]{2,1,0:T(8,128)S(1)} %shard_map.121.both_ref, f32[59,2048]{1,0:T(8,128)S(1)} %copy-done, f32[59,2048]{1,0:T(8,128)S(1)} %copy-done.1), custom_call_target="tpu_custom_call" | custom-call | tf_op jit(solution)/shard_map/pallas_call | solution.py:619
Async XLA Ops:
  0.6 51.4 %copy-start = (f32[59,2048]{1,0:T(8,128)S(1)}, f32[59,2048]{1,0:T(8,128)}, u32[]{:S(2)}) copy-start(f32[59,2048]{1,0:T(8,128)} %params_ref.1) | copy-start | bytes 1449988
  0.6 51.4 %copy-start.1 = (f32[59,2048]{1,0:T(8,128)S(1)}, f32[59,2048]{1,0:T(8,128)}, u32[]{:S(2)}) copy-start(f32[59,2048]{1,0:T(8,128)} %first_ref.1) | copy-start | bytes 1449988

commit v8 on v7

--- a/solution.py
+++ b/solution.py
@@ -55,12 +55,7 @@
     ]
 
 
-def project(values, cam):
-    m = [[cam[3 * r + c] for c in range(3)] for r in range(3)]
-    viewed = [m[r][0] * values[0] + m[r][1] * values[1] + m[r][2] * values[2] + cam[9 + r] for r in range(3)]
-    inverse_z = 1.0 / viewed[2]
-    centre_u = FOCAL * viewed[0] * inverse_z + CENTRE_U
-    centre_v = FOCAL * viewed[1] * inverse_z + CENTRE_V
+def shape_of(values):
     scales = [jnp.exp(values[3 + c]) for c in range(3)]
     norm = jnp.sqrt(values[6] * values[6] + values[7] * values[7] + values[8] * values[8] + values[9] * values[9])
     inverse_norm = 1.0 / norm
@@ -70,6 +65,16 @@
         [2.0 * (x * y + w * z), 1.0 - 2.0 * (x * x + z * z), 2.0 * (y * z - w * x)],
         [2.0 * (x * z - w * y), 2.0 * (y * z + w * x), 1.0 - 2.0 * (x * x + y * y)],
     ]
+    return rot, scales, -jnp.log(1.0 + jnp.exp(-values[10]))
+
+
+def project(values, cam, shape=None):
+    rot, scales, log_opacity = shape_of(values) if shape is None else shape
+    m = [[cam[3 * r + c] for c in range(3)] for r in range(3)]
+    viewed = [m[r][0] * values[0] + m[r][1] * values[1] + m[r][2] * values[2] + cam[9 + r] for r in range(3)]
+    inverse_z = 1.0 / viewed[2]
+    centre_u = FOCAL * viewed[0] * inverse_z + CENTRE_U
+    centre_v = FOCAL * viewed[1] * inverse_z + CENTRE_V
     focal_z = FOCAL * inverse_z
     jac = [[focal_z * (m[r][c] - viewed[r] * inverse_z * m[2][c]) for c in range(3)] for r in range(2)]
     proj = [
@@ -80,7 +85,6 @@
     cov_xy = proj[0][0] * proj[1][0] + proj[0][1] * proj[1][1] + proj[0][2] * proj[1][2]
     cov_yy = proj[1][0] * proj[1][0] + proj[1][1] * proj[1][1] + proj[1][2] * proj[1][2] + 0.3
     inverse_det = 1.0 / (cov_xx * cov_yy - cov_xy * cov_xy)
-    log_opacity = -jnp.log(1.0 + jnp.exp(-values[10]))
     inverse_distance = 1.0 / jnp.sqrt(viewed[0] * viewed[0] + viewed[1] * viewed[1] + viewed[2] * viewed[2])
     terms = harmonics(*[viewed[c] * inverse_distance for c in range(3)])
     colour = []
@@ -199,8 +203,8 @@
     return out
 
 
-def owner_forward(cam_ref, pick, image_of, weave, par3, shown3, put):
-    shown = project([par3[c] for c in range(59)], cameras_of(cam_ref, image_of))
+def owner_forward(cam_ref, pick, image_of, weave, par3, shown3, shape, put):
+    shown = project([par3[c] for c in range(59)], cameras_of(cam_ref, image_of), shape)
     for q in range(9):
         shown3[q] = shown[q]
     for q in range(9, 16):
@@ -458,12 +462,12 @@
     mesh_ids = pl.DeviceIdType.MESH
 
     barrier = pltpu.get_barrier_semaphore()
+    @pl.loop(1, 64, unroll=9)
+    def _(s):
+        pl.semaphore_signal(barrier, inc=1, device_id=(i, lax.rem(j + s, 64)), device_id_type=mesh_ids)
+
     for s in range(1, 8):
         pl.semaphore_signal(barrier, inc=1, device_id=(lax.rem(i + s, 8), j), device_id_type=mesh_ids)
-
-    @pl.loop(1, 64)
-    def _(s):
-        pl.semaphore_signal(barrier, inc=1, device_id=(i, lax.rem(j + s, 64)), device_id_type=mesh_ids)
 
     loads = [
         pltpu.make_async_copy(source, target, in_sems.at[c])
@@ -517,15 +521,16 @@
     to_img(lambda t: cam_row.at[pl.ds(0, 1)], cams.at[pl.ds(i, 1)], 0)
     loads[1].wait()
     owner_tables(send_ref, pick, image_of, weave)
+    for load in loads[2:10]:
+        load.wait()
+    shape = shape_of([par3[c] for c in range(59)])
     landed(cams.at[pl.ds(0, 7)], recv_sems.at[0])
 
     def put_shown(x):
         for r in range(3):
             shown_out[:, r, :] = x[64 * r:64 * (r + 1)]
 
-    for load in loads[2:10]:
-        load.wait()
-    owner_forward(cams, pick, image_of, weave, par3, shown3, put_shown)
+    owner_forward(cams, pick, image_of, weave, par3, shown3, shape, put_shown)
     to_dev(shown_out, shown_mid, 1)
     for load in loads[10:]:
         load.wait()

time: 53.6 us -> 53.4 us (level)
  no operation moved by 1% of the time
where the time goes in v8:
time: 53.4 us; the launch traced here: 53.3 us
  Pallas kernels  52.6 us (99%)
  between operations  0.67 us (1%)
    pallas_call x1, Pallas kernels, local(): pl.pallas_call(step, out_shape=jax.ShapeDtypeStruct((2, 59, 2048), F32),...  51.2 us
    pallas_call x1, Pallas kernels, local(): pl.pallas_call(adam, out_shape=(shape, shape, shape), in_specs=[vmem] * 3...  1.38 us

profile of v8, /device:TPU:1, one launch (start us, length us, event | category | flops | bytes accessed | tf_op | source)
XLA Modules:
  0.0 53.3 jit_solution(12305131423481629513)
XLA Ops:
  0.6 0.0 copy-start
  0.6 0.0 copy-start.1
  0.7 51.2 %shard_map.121.both_ref = f32[2,59,2048]{2,1,0:T(8,128)S(1)} custom-call(f32[59,2048]{1,0:T(8,128)} %params_ref.1, s32[1,512]{1,0:T(1,128)} %send_hbm.1, s32[1,512]{1,0:T(1,128)} %bitcast.5, s32[8,256]{1,0:T(8,128)} %bitcast.4, s32[1,8]{1,0:T(1,128)} %where_hbm.1, s32[1,8]{1,0:T(1,128)} %live_hbm.1, f32[8,768]{1,0:T(8,128)} %bitcast.3, f32[1,12]{1,0:T(1,128)} %camera_hbm.1, ...), custom_call_target="tpu_custom_call" | custom-call | tf_op jit(solution)/shard_map/pallas_call | solution.py:600
  51.9 0.0 copy-done
  51.9 0.0 copy-done.1
  51.9 1.4 %shard_map.122 = (f32[59,2048]{1,0:T(8,128)}, f32[59,2048]{1,0:T(8,128)}, f32[59,2048]{1,0:T(8,128)}) custom-call(f32[2,59,2048]{2,1,0:T(8,128)S(1)} %shard_map.121.both_ref, f32[59,2048]{1,0:T(8,128)S(1)} %copy-done, f32[59,2048]{1,0:T(8,128)S(1)} %copy-done.1), custom_call_target="tpu_custom_call" | custom-call | tf_op jit(solution)/shard_map/pallas_call | solution.py:624
Async XLA Ops:
  0.6 51.2 %copy-start = (f32[59,2048]{1,0:T(8,128)S(1)}, f32[59,2048]{1,0:T(8,128)}, u32[]{:S(2)}) copy-start(f32[59,2048]{1,0:T(8,128)} %params_ref.1) | copy-start | bytes 1449988
  0.6 51.2 %copy-start.1 = (f32[59,2048]{1,0:T(8,128)S(1)}, f32[59,2048]{1,0:T(8,128)}, u32[]{:S(2)}) copy-start(f32[59,2048]{1,0:T(8,128)} %first_ref.1) | copy-start | bytes 1449988

commit v9 on v8

--- a/solution.py
+++ b/solution.py
@@ -334,7 +334,7 @@
         sorted_parts = nn(jnp.concatenate(pieces(mine, 3), axis=0), sort[n])
         front = fold(sorted_parts, 3)
         front3[n] = jnp.where(iota((8, 256), 0) < 3, pltpu.roll(front, 10, 0)[0:8], 0.0)
-        alpha = jnp.exp2(nn(power[...], sorted_parts.astype(BF16)))
+        alpha = jnp.minimum(jnp.exp2(nn(power[...], sorted_parts.astype(BF16))), 0.9999999)
         alpha3[n] = alpha
         split3[n] = jnp.concatenate(pieces(jnp.log(1.0 - alpha), 2), axis=1)
     for n in range(8):

time: 53.4 us -> 53.4 us (level)
  no operation moved by 1% of the time
where the time goes in v9:
time: 53.4 us; the launch traced here: 53.3 us
  Pallas kernels  52.6 us (99%)
  between operations  0.67 us (1%)
    pallas_call x1, Pallas kernels, local(): pl.pallas_call(step, out_shape=jax.ShapeDtypeStruct((2, 59, 2048), F32),...  51.2 us
    pallas_call x1, Pallas kernels, local(): pl.pallas_call(adam, out_shape=(shape, shape, shape), in_specs=[vmem] * 3...  1.38 us

profile of v9, /device:TPU:1, one launch (start us, length us, event | category | flops | bytes accessed | tf_op | source)
XLA Modules:
  0.0 53.3 jit_solution(13568184815313238421)
XLA Ops:
  0.6 0.0 copy-start
  0.6 0.0 copy-start.1
  0.7 51.2 %shard_map.121.both_ref = f32[2,59,2048]{2,1,0:T(8,128)S(1)} custom-call(f32[59,2048]{1,0:T(8,128)} %params_ref.1, s32[1,512]{1,0:T(1,128)} %send_hbm.1, s32[1,512]{1,0:T(1,128)} %bitcast.5, s32[8,256]{1,0:T(8,128)} %bitcast.4, s32[1,8]{1,0:T(1,128)} %where_hbm.1, s32[1,8]{1,0:T(1,128)} %live_hbm.1, f32[8,768]{1,0:T(8,128)} %bitcast.3, f32[1,12]{1,0:T(1,128)} %camera_hbm.1, ...), custom_call_target="tpu_custom_call" | custom-call | tf_op jit(solution)/shard_map/pallas_call | solution.py:600
  51.9 0.0 copy-done
  51.9 0.0 copy-done.1
  51.9 1.4 %shard_map.122 = (f32[59,2048]{1,0:T(8,128)}, f32[59,2048]{1,0:T(8,128)}, f32[59,2048]{1,0:T(8,128)}) custom-call(f32[2,59,2048]{2,1,0:T(8,128)S(1)} %shard_map.121.both_ref, f32[59,2048]{1,0:T(8,128)S(1)} %copy-done, f32[59,2048]{1,0:T(8,128)S(1)} %copy-done.1), custom_call_target="tpu_custom_call" | custom-call | tf_op jit(solution)/shard_map/pallas_call | solution.py:624
Async XLA Ops:
  0.6 51.2 %copy-start = (f32[59,2048]{1,0:T(8,128)S(1)}, f32[59,2048]{1,0:T(8,128)}, u32[]{:S(2)}) copy-start(f32[59,2048]{1,0:T(8,128)} %params_ref.1) | copy-start | bytes 1449988
  0.6 51.2 %copy-start.1 = (f32[59,2048]{1,0:T(8,128)S(1)}, f32[59,2048]{1,0:T(8,128)}, u32[]{:S(2)}) copy-start(f32[59,2048]{1,0:T(8,128)} %first_ref.1) | copy-start | bytes 1449988
